TPU v7x, 32 devices: a whole 2x2x4 slice. The times are simulated.
32 devices in a mesh: shard: 2 (over x), replica: 16 (over z, y, core).
Axes of the slice: x: 2, y: 2, z: 4, core: 2. Of those that a mesh axis runs over, the one named last changes fastest.
Arguments:
- tokens: bfloat16 [32768, 576], P(('shard', 'replica')), may hold values from -6 to 6
- cotangent: bfloat16 [32768, 576], P(('shard', 'replica')), may hold values from -6 to 6
- lengths: int32 [32, 4], P(('shard', 'replica')), may hold values from 0 to 1024, as said below
- attn_gain: bfloat16 [576], P('shard'), may hold values from 0.5 to 1.5
- w_query: bfloat16 [576, 576], P('shard'), may hold values from -0.25 to 0.25
- key_projection: bfloat16 [576, 192], P('shard'), may hold values from -0.25 to 0.25
- value_projection: bfloat16 [576, 192], P('shard'), may hold values from -0.25 to 0.25
- w_out: bfloat16 [576, 576], P('shard'), may hold values from -1 to 1
- mlp_gain: bfloat16 [576], P('shard'), may hold values from 0.5 to 1.5
- w_gate: bfloat16 [576, 1536], P('shard'), may hold values from -0.25 to 0.25
- w_up: bfloat16 [576, 1536], P('shard'), may hold values from -0.25 to 0.25
- w_down: bfloat16 [1536, 576], P('shard'), may hold values from -0.15625 to 0.15625
Outputs:
- block_out: bfloat16 [32768, 576], P(('shard', 'replica'))
- grad_tokens: bfloat16 [32768, 576], P(('shard', 'replica'))
- grad_attn_gain: float32 [576], P('shard')
- grad_query: float32 [576, 576], P('shard')
- grad_key: float32 [576, 192], P('shard')
- grad_value: float32 [576, 192], P('shard')
- grad_out: float32 [576, 576], P('shard')
- grad_mlp_gain: float32 [576], P('shard')
- grad_gate: float32 [576, 1536], P('shard')
- grad_up: float32 [576, 1536], P('shard')
- grad_down: float32 [1536, 576], P('shard')
Inputs may be any that keep to these rules, and one draw needn't show every extreme that they name: `lengths`: each row holds one sequence of 1024 slots; later entries are 0 (empty slots).
All inputs are finite; a program needn't handle non-finite values.
Results may differ from a plain program's by a relative error of at most 0.015.
Values may be sent and summed in bfloat16 or wider, within the bound.
No kernel may reach another device: no remote copies, remote signals or barrier semaphores. Data moves between devices by JAX's collectives and lax.ppermute only.
A program may use at most 192 MiB of HBM per device.

v0:
```python
import math

import jax
import jax.numpy as jnp
from jax import lax
from jax.sharding import PartitionSpec as P

QUERY_HEADS = 9
KEY_VALUE_HEADS = 3
HEAD_SIZE = 64


EPS = 1e-05
THETA = 100000.0


def layout(lens_row, count_of_rows):
    seq_ends = jnp.cumsum(lens_row)
    places = jnp.arange(count_of_rows, dtype=jnp.int32)
    segment = jnp.sum((places[:, None] >= seq_ends[None, :]).astype(jnp.int32), axis=1)
    starts = seq_ends - lens_row
    slot_ids = jnp.arange(lens_row.shape[0], dtype=jnp.int32)
    in_slot = segment[:, None] == slot_ids[None, :]
    seq_start = jnp.sum(jnp.where(in_slot, starts[None, :], 0), axis=1)
    seq_start = seq_start + jnp.where(segment == lens_row.shape[0], seq_ends[-1], 0)
    return (segment, places - seq_start, segment < lens_row.shape[0])


def rotation(token_position, width):
    half_width = width // 2
    inverse = jnp.exp(jnp.arange(half_width, dtype=jnp.float32) * (-2.0 * math.log(THETA) / width))
    angles = token_position.astype(jnp.float32)[:, None] * inverse[None, :]
    cosine_table = jnp.concatenate([jnp.cos(angles), jnp.cos(angles)], -1)[:, None, :]
    sine_table = jnp.concatenate([jnp.sin(angles), jnp.sin(angles)], -1)[:, None, :]
    return (cosine_table, sine_table)


def apply_rotation(vector, cosine_table, sine_table):
    half_width = vector.shape[-1] // 2
    turned = jnp.concatenate([-vector[..., half_width:], vector[..., :half_width]], -1)
    return vector * cosine_table + turned * sine_table


def reverse_rotation(gradient, cosine_table, sine_table):
    half_width = gradient.shape[-1] // 2
    shifted = gradient * sine_table
    return gradient * cosine_table + jnp.concatenate(
        [shifted[..., half_width:], -shifted[..., :half_width]], -1
    )


def normalize(vector, gain_vec):
    return vector * lax.rsqrt(jnp.mean(vector * vector, -1, keepdims=True) + EPS) * gain_vec


def swiglu(gate_part, up_part):
    return jax.nn.silu(gate_part) * up_part


def outer_sum(left, right):
    return lax.dot_general(
        left, right, (((0,), (0,)), ((), ())), preferred_element_type=jnp.float32
    )


def times_transpose(left, right):
    return lax.dot_general(
        left, right, (((1,), (1,)), ((), ())), preferred_element_type=jnp.float32
    )


def masked_scores(query_rows, key_rows, segment, begin_row, finish):
    score_scale = 1.0 / math.sqrt(query_rows.shape[-1])
    scores = (
        jnp.einsum("rha,ka->hrk", query_rows, key_rows, preferred_element_type=jnp.float32)
        * score_scale
    )
    row_ids = begin_row + jnp.arange(finish - begin_row, dtype=jnp.int32)
    key_ids = jnp.arange(finish, dtype=jnp.int32)
    allowed = (segment[begin_row:finish][:, None] == segment[:finish][None, :]) & (
        key_ids[None, :] <= row_ids[:, None]
    )
    return jnp.where(allowed[None], scores, -1e30)


def attend(query_heads, key_heads, value_heads, segment, block_rows):
    count_of_rows = query_heads.shape[0]
    out_parts = []
    lse_parts = []
    for begin_row in range(0, count_of_rows, block_rows):
        finish = begin_row + block_rows
        group_outs = []
        group_lse = []
        for kv_group in range(key_heads.shape[1]):
            scores = masked_scores(
                query_heads[begin_row:finish, kv_group],
                key_heads[:finish, kv_group],
                segment,
                begin_row,
                finish,
            )
            row_max = jnp.max(scores, -1, keepdims=True)
            raised = jnp.exp(scores - row_max)
            row_total = jnp.sum(raised, -1, keepdims=True)
            probability = (raised / row_total).astype(jnp.bfloat16)
            group_outs.append(
                jnp.einsum(
                    "hrk,ka->rha",
                    probability,
                    value_heads[:finish, kv_group],
                    preferred_element_type=jnp.float32,
                )
            )
            group_lse.append((row_max + jnp.log(row_total))[..., 0].T)
        out_parts.append(jnp.stack(group_outs, axis=1))
        lse_parts.append(jnp.stack(group_lse, axis=1))
    return (jnp.concatenate(out_parts, 0), jnp.concatenate(lse_parts, 0))


def attend_back(query_heads, key_heads, value_heads, segment, log_totals, grad_heads, block_rows):
    count_of_rows = query_heads.shape[0]
    score_scale = 1.0 / math.sqrt(query_heads.shape[-1])
    grad_keys = jnp.zeros(key_heads.shape, jnp.float32)
    grad_value_heads = jnp.zeros(value_heads.shape, jnp.float32)
    query_parts = []
    for begin_row in range(0, count_of_rows, block_rows):
        finish = begin_row + block_rows
        group_grads = []
        for kv_group in range(key_heads.shape[1]):
            query_rows = query_heads[begin_row:finish, kv_group]
            grad_rows = grad_heads[begin_row:finish, kv_group]
            scores = masked_scores(
                query_rows, key_heads[:finish, kv_group], segment, begin_row, finish
            )
            probability = jnp.exp(scores - log_totals[begin_row:finish, kv_group].T[..., None])
            grad_probs = jnp.einsum(
                "rha,ka->hrk",
                grad_rows,
                value_heads[:finish, kv_group],
                preferred_element_type=jnp.float32,
            )
            row_delta = jnp.sum(probability * grad_probs, -1, keepdims=True)
            grad_scores = (probability * (grad_probs - row_delta)).astype(jnp.bfloat16)
            group_grads.append(
                jnp.einsum(
                    "hrk,ka->rha",
                    grad_scores,
                    key_heads[:finish, kv_group],
                    preferred_element_type=jnp.float32,
                )
                * score_scale
            )
            key_part = (
                jnp.einsum(
                    "hrk,rha->ka", grad_scores, query_rows, preferred_element_type=jnp.float32
                )
                * score_scale
            )
            value_part = jnp.einsum(
                "hrk,rha->ka",
                probability.astype(jnp.bfloat16),
                grad_rows,
                preferred_element_type=jnp.float32,
            )
            grad_keys = grad_keys.at[:finish, kv_group].add(key_part)
            grad_value_heads = grad_value_heads.at[:finish, kv_group].add(value_part)
        query_parts.append(jnp.stack(group_grads, axis=1))
    return (jnp.concatenate(query_parts, 0), grad_keys, grad_value_heads)


def project_attention(
    source, gain_vec, query_w, key_matrix, value_matrix, cosine_table, sine_table
):
    count_of_rows = source.shape[0]
    first_normed_input = normalize(source, gain_vec).astype(jnp.bfloat16)
    query_heads = jnp.dot(first_normed_input, query_w, preferred_element_type=jnp.float32).reshape(
        count_of_rows, QUERY_HEADS, HEAD_SIZE
    )
    query_heads = (
        apply_rotation(query_heads, cosine_table, sine_table)
        .astype(jnp.bfloat16)
        .reshape(count_of_rows, KEY_VALUE_HEADS, QUERY_HEADS // KEY_VALUE_HEADS, HEAD_SIZE)
    )
    key_heads = jnp.dot(first_normed_input, key_matrix, preferred_element_type=jnp.float32).reshape(
        count_of_rows, KEY_VALUE_HEADS, HEAD_SIZE
    )
    key_heads = apply_rotation(key_heads, cosine_table, sine_table).astype(jnp.bfloat16)
    value_heads = (
        jnp.dot(first_normed_input, value_matrix, preferred_element_type=jnp.float32)
        .astype(jnp.bfloat16)
        .reshape(count_of_rows, KEY_VALUE_HEADS, HEAD_SIZE)
    )
    return (first_normed_input, query_heads, key_heads, value_heads)


def project_mlp(middle, gain_vec, gate_w, up_w):
    normed_two = normalize(middle, gain_vec).astype(jnp.bfloat16)
    gate = jnp.dot(normed_two, gate_w, preferred_element_type=jnp.float32)
    up_act = jnp.dot(normed_two, up_w, preferred_element_type=jnp.float32)
    hidden = swiglu(gate, up_act).astype(jnp.bfloat16)
    return (normed_two, gate, up_act, hidden)


def local(
    tokens,
    cotangent,
    lengths,
    attn_gain,
    w_query,
    key_projection,
    value_projection,
    w_out,
    mlp_gain,
    w_gate,
    w_up,
    w_down,
):
    gathered = (
        lax.all_gather(attn_gain, "shard", axis=0, tiled=True),
        lax.all_gather(w_query, "shard", axis=0, tiled=True),
        lax.all_gather(key_projection, "shard", axis=0, tiled=True),
        lax.all_gather(value_projection, "shard", axis=0, tiled=True),
        lax.all_gather(w_out, "shard", axis=0, tiled=True),
        lax.all_gather(mlp_gain, "shard", axis=0, tiled=True),
        lax.all_gather(w_gate, "shard", axis=0, tiled=True),
        lax.all_gather(w_up, "shard", axis=0, tiled=True),
        lax.all_gather(w_down, "shard", axis=0, tiled=True),
    )
    gain_one, query_w, key_matrix, value_matrix, out_w, gain_two, gate_w, up_w, down_w = gathered
    count_of_rows = tokens.shape[0]
    block_rows = min(512, count_of_rows)
    segment, token_position, valid = layout(lengths[0], count_of_rows)
    valid_col = valid.astype(jnp.float32)[:, None]
    cosine_table, sine_table = rotation(token_position, HEAD_SIZE)
    source = tokens.astype(jnp.float32)
    first_normed_input, query_heads, key_heads, value_heads = project_attention(
        source,
        gain_one.astype(jnp.float32),
        query_w,
        key_matrix,
        value_matrix,
        cosine_table,
        sine_table,
    )
    attn_rows, log_totals = attend(query_heads, key_heads, value_heads, segment, block_rows)
    heads = attn_rows.reshape(count_of_rows, QUERY_HEADS * HEAD_SIZE).astype(jnp.bfloat16)
    middle = source + jnp.dot(heads, out_w, preferred_element_type=jnp.float32)
    normed_two, gate, up_act, hidden = project_mlp(
        middle, gain_two.astype(jnp.float32), gate_w, up_w
    )
    result = middle + jnp.dot(hidden, down_w, preferred_element_type=jnp.float32)
    block_out = (result * valid_col).astype(jnp.bfloat16)
    back_weights = (
        lax.all_gather(attn_gain, "shard", axis=0, tiled=True),
        lax.all_gather(w_query, "shard", axis=0, tiled=True),
        lax.all_gather(key_projection, "shard", axis=0, tiled=True),
        lax.all_gather(value_projection, "shard", axis=0, tiled=True),
        lax.all_gather(w_out, "shard", axis=0, tiled=True),
        lax.all_gather(mlp_gain, "shard", axis=0, tiled=True),
        lax.all_gather(w_gate, "shard", axis=0, tiled=True),
        lax.all_gather(w_up, "shard", axis=0, tiled=True),
        lax.all_gather(w_down, "shard", axis=0, tiled=True),
    )
    gain_one, query_w, key_matrix, value_matrix, out_w, gain_two, gate_w, up_w, down_w = (
        back_weights
    )
    gain_first = gain_one.astype(jnp.float32)
    gain_second = gain_two.astype(jnp.float32)
    first_normed_input, query_heads, key_heads, value_heads = project_attention(
        source, gain_first, query_w, key_matrix, value_matrix, cosine_table, sine_table
    )
    middle = source + jnp.dot(heads, out_w, preferred_element_type=jnp.float32)
    normed_two, gate, up_act, hidden = project_mlp(middle, gain_second, gate_w, up_w)
    grad_result = cotangent.astype(jnp.float32) * valid_col
    grad_result_low = grad_result.astype(jnp.bfloat16)
    grad_down_w = outer_sum(hidden, grad_result_low)
    grad_hidden = times_transpose(grad_result_low, down_w)
    unused_act, pull_mlp = jax.vjp(swiglu, gate, up_act)
    grad_gate_act, grad_up_act = pull_mlp(grad_hidden)
    grad_gate_act = grad_gate_act.astype(jnp.bfloat16)
    grad_up_act = grad_up_act.astype(jnp.bfloat16)
    grad_gate_w = outer_sum(normed_two, grad_gate_act)
    grad_up_w = outer_sum(normed_two, grad_up_act)
    grad_normed_two = times_transpose(grad_gate_act, gate_w) + times_transpose(grad_up_act, up_w)
    unused_two, pull_two = jax.vjp(normalize, middle, gain_second)
    grad_middle_part, grad_gain_two = pull_two(grad_normed_two)
    grad_middle = grad_result + grad_middle_part
    grad_branch = grad_middle.astype(jnp.bfloat16)
    grad_out_w = outer_sum(heads, grad_branch)
    grad_heads = (
        times_transpose(grad_branch, out_w)
        .astype(jnp.bfloat16)
        .reshape(count_of_rows, KEY_VALUE_HEADS, QUERY_HEADS // KEY_VALUE_HEADS, HEAD_SIZE)
    )
    grad_rot_q, grad_rotated_key, grad_value_heads = attend_back(
        query_heads, key_heads, value_heads, segment, log_totals, grad_heads, block_rows
    )
    grad_q = (
        reverse_rotation(
            grad_rot_q.reshape(count_of_rows, QUERY_HEADS, HEAD_SIZE), cosine_table, sine_table
        )
        .reshape(count_of_rows, QUERY_HEADS * HEAD_SIZE)
        .astype(jnp.bfloat16)
    )
    grad_k = (
        reverse_rotation(grad_rotated_key, cosine_table, sine_table)
        .reshape(count_of_rows, KEY_VALUE_HEADS * HEAD_SIZE)
        .astype(jnp.bfloat16)
    )
    grad_value_rows = grad_value_heads.reshape(count_of_rows, KEY_VALUE_HEADS * HEAD_SIZE).astype(
        jnp.bfloat16
    )
    grad_query_w = outer_sum(first_normed_input, grad_q)
    grad_key_w = outer_sum(first_normed_input, grad_k)
    grad_value_w = outer_sum(first_normed_input, grad_value_rows)
    grad_normed_one = (
        times_transpose(grad_q, query_w)
        + times_transpose(grad_k, key_matrix)
        + times_transpose(grad_value_rows, value_matrix)
    )
    unused_one, pull_one = jax.vjp(normalize, source, gain_first)
    grad_source_part, grad_gain_one = pull_one(grad_normed_one)
    grad_tokens = (grad_middle + grad_source_part).astype(jnp.bfloat16)
    owned = (
        lax.psum_scatter(
            grad_gain_one.astype(jnp.bfloat16), "shard", scatter_dimension=0, tiled=True
        ).astype(jnp.float32),
        lax.psum_scatter(
            grad_query_w.astype(jnp.bfloat16), "shard", scatter_dimension=0, tiled=True
        ).astype(jnp.float32),
        lax.psum_scatter(
            grad_key_w.astype(jnp.bfloat16), "shard", scatter_dimension=0, tiled=True
        ).astype(jnp.float32),
        lax.psum_scatter(
            grad_value_w.astype(jnp.bfloat16), "shard", scatter_dimension=0, tiled=True
        ).astype(jnp.float32),
        lax.psum_scatter(
            grad_out_w.astype(jnp.bfloat16), "shard", scatter_dimension=0, tiled=True
        ).astype(jnp.float32),
        lax.psum_scatter(
            grad_gain_two.astype(jnp.bfloat16), "shard", scatter_dimension=0, tiled=True
        ).astype(jnp.float32),
        lax.psum_scatter(
            grad_gate_w.astype(jnp.bfloat16), "shard", scatter_dimension=0, tiled=True
        ).astype(jnp.float32),
        lax.psum_scatter(
            grad_up_w.astype(jnp.bfloat16), "shard", scatter_dimension=0, tiled=True
        ).astype(jnp.float32),
        lax.psum_scatter(
            grad_down_w.astype(jnp.bfloat16), "shard", scatter_dimension=0, tiled=True
        ).astype(jnp.float32),
    )
    totals = lax.psum(
        (owned[0], owned[1], owned[2], owned[3], owned[4], owned[5], owned[6], owned[7], owned[8]),
        "replica",
    )
    return (
        block_out,
        grad_tokens,
        totals[0],
        totals[1],
        totals[2],
        totals[3],
        totals[4],
        totals[5],
        totals[6],
        totals[7],
        totals[8],
    )


def solution(mesh):
    placed = (
        P(("shard", "replica"), None),
        P(("shard", "replica"), None),
        P(("shard", "replica"), None),
        P("shard"),
        P("shard", None),
        P("shard", None),
        P("shard", None),
        P("shard", None),
        P("shard"),
        P("shard", None),
        P("shard", None),
        P("shard", None),
    )
    return jax.shard_map(
        local,
        mesh=mesh,
        in_specs=placed,
        out_specs=(
            P(("shard", "replica"), None),
            P(("shard", "replica"), None),
            P("shard"),
            P("shard", None),
            P("shard", None),
            P("shard", None),
            P("shard", None),
            P("shard"),
            P("shard", None),
            P("shard", None),
            P("shard", None),
        ),
        check_vma=False,
    )
```

profile of v0, /device:TPU:1, one launch (start us, length us, event | category | flops | bytes accessed | tf_op | source)
XLA Modules:
  0.0 561.8 jit_solution(15622030943561490132)
XLA Ops:
  12.2 4.3 all-reduce.8
  17.2 7.4 %all_gather.38 = bf16[576,192]{1,0:T(8,128)(2,1)S(1)} all-gather(bf16[288,192]{1,0:T(8,128)(2,1)S(1)} %copy-done.65), channel_id=1, replica_groups=mesh['shard'=2,'replica'=16] {'shard'}, dimensions={0}, use_global_device_ids=true | all-gather | bytes 331776 | tf_op jit(solution)/shard_map/all_gather | solution.py:221
  24.6 19.0 %all_gather.39 = bf16[576,576]{1,0:T(8,128)(2,1)S(1)} all-gather(bf16[288,576]{1,0:T(8,128)(2,1)S(1)} %copy-done.63), channel_id=1, replica_groups=mesh['shard'=2,'replica'=16] {'shard'}, dimensions={0}, use_global_device_ids=true | all-gather | bytes 995328 | tf_op jit(solution)/shard_map/all_gather | solution.py:220
  49.8 5.0 all_gather.37
  69.9 17.7 %all_gather.40 = bf16[576,576]{1,0:T(8,128)(2,1)S(1)} all-gather(bf16[288,576]{1,0:T(8,128)(2,1)S(1)} %copy-done.64), channel_id=1, replica_groups=mesh['shard'=2,'replica'=16] {'shard'}, dimensions={0}, use_global_device_ids=true | all-gather | bytes 995328 | tf_op jit(solution)/shard_map/all_gather | solution.py:223
  96.0 7.2 %fusion.195 = f32[1024,1536]{1,0:T(8,128)} fusion(bf16[1024,576]{0,1:T(8,128)(2,1)} %multiply_convert_fusion.3, bf16[576,1536]{1,0:T(8,128)(2,1)} %all-gather.6.cloned.1.call-done), kind=kOutput, calls=%fused_computation.296 | convolution fusion | flops 1811939328 | bytes 9240576 | tf_op jit(solution)/shard_map/dot_general | solution.py:199
  103.2 7.2 %fusion.194 = f32[1024,1536]{1,0:T(8,128)} fusion(bf16[1024,576]{0,1:T(8,128)(2,1)} %multiply_convert_fusion.3, bf16[576,1536]{1,0:T(8,128)(2,1)} %all-gather.4.cloned.1.call-done), kind=kOutput, calls=%fused_computation.295 | convolution fusion | flops 1811939328 | bytes 9240576 | tf_op jit(solution)/shard_map/dot_general | solution.py:198
  110.4 10.8 %all-gather.8.cloned.1.call-done = bf16[1536,576]{0,1:T(8,128)(2,1)} async-done(((bf16[768,576]{0,1:T(8,128)(2,1)}), bf16[1536,576]{0,1:T(8,128)(2,1)}) %all-gather.8.cloned.1.call-update) | async-done | bytes 1769488 | tf_op jit(solution)/shard_map/all_gather | solution.py:227
  121.2 11.5 %multiply_convert_fusion = (bf16[1024,1536]{1,0:T(8,128)(2,1)S(1)}, bf16[1024,1536]{1,0:T(8,128)(2,1)S(1)}, bf16[1024,1536]{1,0:T(8,128)(2,1)}) fusion(f32[1024,1536]{1,0:T(8,128)} %fusion.194, f32[1024,1536]{1,0:T(8,128)} %fusion.195, bf16[1536,576]{0,1:T(8,128)(2,1)} %all-gather.8.cloned.1.call-done, bf16[1024,576]{0,1:T(8,128)(2,1)} %param.37, ...), kind=kOutput, calls=%fused_computation.25 | convolution fusion | flops 1838874624 | bytes 24973312 | tf_op jit(solution)/shard_map/dot_general | solution.py:67
  137.2 2.9 multiply_reduce_fusion
  142.3 2.1 copy-done.9
  145.0 2.3 fusion.31
  147.3 2.3 fusion.25
  149.9 2.3 fusion.28
  155.1 3.0 scatter-add.51
  158.2 4.4 fusion.144
  162.6 3.0 scatter-add.54
  165.6 6.8 %fusion.9 = (f32[3,512]{1,0:T(4,128)S(1)}, f32[1024,512,3]{1,0,2:T(8,128)}) fusion(f32[3,512,1024]{1,2,0:T(8,128)} %copy-done, f32[3,512]{1,0:T(4,128)S(1)} %log_add_fusion.2, bf16[1024,3,3,64]{0,3,2,1:T(8,128)(2,1)} %bitcast.489, bf16[1024,3,64]{0,2,1:T(8,128)(2,1)S(1)} %bitcast.514), kind=kOutput, calls=%fused_computation.16 | convolution fusion | flops 206043648 | bytes 12924928 | tf_op jit(solution)/shard_map/rha,ka->hrk/dot_general | solution.py:136
  172.5 2.9 fusion.90
  175.4 6.8 %fusion.6 = (f32[3,512]{1,0:T(4,128)S(1)}, f32[1024,512,3]{1,0,2:T(8,128)}) fusion(f32[3,512,1024]{1,2,0:T(8,128)} %copy-done.2, f32[3,512]{1,0:T(4,128)S(1)} %log_add_fusion.1, bf16[1024,3,3,64]{0,3,2,1:T(8,128)(2,1)S(1)} %bitcast.491, bf16[1024,3,64]{0,2,1:T(8,128)(2,1)S(1)} %bitcast.515), kind=kOutput, calls=%fused_computation.11 | convolution fusion | flops 206043648 | bytes 12924928 | tf_op jit(solution)/shard_map/rha,ka->hrk/dot_general | solution.py:136
  182.2 2.7 fusion.99
  184.9 3.9 fusion.3
  188.9 2.8 fusion.108
  195.2 2.9 fusion.33
  200.9 3.9 fusion.153
  205.7 2.6 scatter-add.41
  208.3 3.3 fusion.150
  211.5 2.3 scatter-add.44
  213.9 6.7 %fusion.5 = bf16[3,512,1024]{1,2,0:T(8,128)(2,1)S(1)} fusion(f32[1024,512,3]{1,0,2:T(8,128)} %get-tuple-element.209, f32[3,512,1024]{1,2,0:T(8,128)} %copy-done.1, f32[3,512]{1,0:T(4,128)S(1)} %get-tuple-element.208, f32[3,512]{1,0:T(4,128)S(1)} %log_add_fusion), kind=kLoop, calls=%fused_computation.8 | loop fusion | flops 6291456 | bytes 15740928 | tf_op jit(solution)/shard_map/convert_element_type | solution.py:143
  220.6 2.3 fusion.72
  222.9 4.7 fusion.8
  227.6 2.5 fusion.73
  230.1 4.7 fusion.11
  241.6 2.6 fusion.75
  244.2 2.3 fusion.74
  246.6 2.6 fusion.76
  249.2 4.1 convolution_convert_fusion.4
  260.5 5.5 convolution_convert_fusion
  266.1 5.3 convolution_convert_fusion.2
  271.6 5.2 convolution_convert_fusion.1
  279.8 3.0 fusion.49
  282.8 4.5 all-reduce.7
  290.0 3.5 fusion.52
  293.5 4.9 multiply_convert_fusion.2
  298.5 30.3 %reduce-scatter.20.cloned.1.call-done = bf16[768,576]{0,1:T(8,128)(2,1)} async-done(((bf16[1536,576]{0,1:T(8,128)(2,1)}), bf16[768,576]{0,1:T(8,128)(2,1)}) %reduce-scatter.20.cloned.1.call-update) | async-done | bytes 884752 | tf_op jit(solution)/shard_map/reduce_scatter | solution.py:349
  328.7 31.2 %reduce-scatter.16.cloned.1.call-done = bf16[288,1536]{1,0:T(8,128)(2,1)} async-done(((bf16[576,1536]{1,0:T(8,128)(2,1)}), bf16[288,1536]{1,0:T(8,128)(2,1)}) %reduce-scatter.16.cloned.1.call-update) | async-done | bytes 884752 | tf_op jit(solution)/shard_map/reduce_scatter | solution.py:343
  359.9 30.9 %reduce-scatter.18.cloned.1.call-done = bf16[288,1536]{1,0:T(8,128)(2,1)} async-done(((bf16[576,1536]{1,0:T(8,128)(2,1)}), bf16[288,1536]{1,0:T(8,128)(2,1)}) %reduce-scatter.18.cloned.1.call-update) | async-done | bytes 884752 | tf_op jit(solution)/shard_map/reduce_scatter | solution.py:346
  390.9 163.6 %all-reduce.10 = (f32[288]{0:T(512)}, f32[288,576]{1,0:T(8,128)}, f32[288,192]{1,0:T(8,128)}, f32[288,192]{1,0:T(8,128)}, f32[288,576]{1,0:T(8,128)}, /*index=5*...) all-reduce(f32[288]{0:T(512)S(1)} %copy-done.71, ...), channel_id=1, replica_groups=mesh['shard'=2,'replica'=16] {'replica'}, use_global_device_ids=true, to_apply=%region_28.29 | all-reduce | flops 1770048 | bytes 10621440 | tf_op jit(solution)/shard_map/psum | solution.py:353
  (311 shorter events, 70.7 us)
Async XLA Ops:
  7.2 9.4 %copy-start.21 = (bf16[1024,576]{0,1:T(8,128)(2,1)S(1)}, bf16[1024,576]{0,1:T(8,128)(2,1)}, u32[]{:S(2)}) copy-start(bf16[1024,576]{0,1:T(8,128)(2,1)} %param.36) | copy-start | bytes 3538948
  7.2 9.9 %copy-start.65 = (bf16[288,192]{1,0:T(8,128)(2,1)S(1)}, bf16[288,192]{1,0:T(8,128)(2,1)}, u32[]{:S(2)}) copy-start(bf16[288,192]{1,0:T(8,128)(2,1)} %param.41) | copy-start | bytes 331780
  7.2 17.4 %copy-start.63 = (bf16[288,576]{1,0:T(8,128)(2,1)S(1)}, bf16[288,576]{1,0:T(8,128)(2,1)}, u32[]{:S(2)}) copy-start(bf16[288,576]{1,0:T(8,128)(2,1)} %param.40) | copy-start | bytes 995332
  7.3 88.8 %all-gather.6.cloned.1.call-start = ((), (), s32[]{:S(2)}) async-start(), calls=%async_computation.8 | async-start | bytes 2654208 | tf_op jit(solution)/shard_map/all_gather | solution.py:226
  8.0 95.3 %all-gather.4.cloned.1.call-start = ((), (), s32[]{:S(2)}) async-start(), calls=%async_computation.7 | async-start | bytes 2654208 | tf_op jit(solution)/shard_map/all_gather | solution.py:225
  8.7 112.4 %all-gather.8.cloned.1.call-start = ((), (), s32[]{:S(2)}) async-start(), calls=%async_computation.9 | async-start | bytes 2654208 | tf_op jit(solution)/shard_map/all_gather | solution.py:227
  9.5 289.0 %reduce-scatter.12.cloned.1.call-start = ((), (), s32[]{:S(2)}) async-start(), calls=%async_computation.12 | async-start | bytes 442368 | tf_op jit(solution)/shard_map/reduce_scatter | solution.py:334
  10.4 250.0 %copy-start.69 = (f32[1024]{0:T(1024)}, f32[1024]{0:T(1024)S(1)}, u32[]{:S(2)}) copy-start(f32[1024]{0:T(1024)S(1)} %compare_convert_fusion) | copy-start | bytes 12292
  16.9 27.4 %copy-start.67 = (f32[1024]{0:T(1024)}, f32[1024]{0:T(1024)S(1)}, u32[]{:S(2)}) copy-start(f32[1024]{0:T(1024)S(1)} %fusion.53) | copy-start | bytes 12292
  24.6 19.6 %copy-start.47 = (bf16[576,192]{1,0:T(8,128)(2,1)}, bf16[576,192]{1,0:T(8,128)(2,1)S(1)}, u32[]{:S(2)}) copy-start(bf16[576,192]{1,0:T(8,128)(2,1)S(1)} %all_gather.38) | copy-start | bytes 663556
  47.3 20.2 %copy-start.38 = (bf16[1024,3,64]{0,2,1:T(8,128)(2,1)}, bf16[1024,3,64]{0,2,1:T(8,128)(2,1)S(1)}, u32[]{:S(2)}) copy-start(bf16[1024,3,64]{0,2,1:T(8,128)(2,1)S(1)} %fusion.161) | copy-start | bytes 1179652
  48.0 19.6 %copy-start.34 = (bf16[1024,3,3,64]{0,3,2,1:T(8,128)(2,1)}, bf16[1024,3,3,64]{0,3,2,1:T(8,128)(2,1)S(1)}, u32[]{:S(2)}) copy-start(bf16[1024,3,3,64]{0,3,2,1:T(8,128)(2,1)S(1)} %fusion.56) | copy-start | bytes 3538948
  48.7 98.6 %copy-start.3 = (f32[3,512,512]{1,2,0:T(8,128)}, f32[3,512,512]{1,2,0:T(8,128)S(1)}, u32[]{:S(2)}) copy-start(f32[3,512,512]{1,2,0:T(8,128)S(1)} %get-tuple-element.200) | copy-start | bytes 9437188
  48.7 6.7 %copy-start.22 = (bf16[1024,576]{0,1:T(8,128)(2,1)S(1)}, bf16[1024,576]{0,1:T(8,128)(2,1)}, u32[]{:S(2)}) copy-start(bf16[1024,576]{0,1:T(8,128)(2,1)} %param.36) | copy-start | bytes 3538948
  49.8 7.9 %copy-start.5 = (f32[3,512,512]{1,2,0:T(8,128)}, f32[3,512,512]{1,2,0:T(8,128)S(1)}, u32[]{:S(2)}) copy-start(f32[3,512,512]{1,2,0:T(8,128)S(1)} %get-tuple-element.202) | copy-start | bytes 9437188
  56.0 34.5 %copy-start.56 = (bf16[1024,192]{0,1:T(8,128)(2,1)}, bf16[1024,192]{0,1:T(8,128)(2,1)S(1)}, u32[]{:S(2)}) copy-start(bf16[1024,192]{0,1:T(8,128)(2,1)S(1)} %convolution_convert_fusion.6) | copy-start | bytes 1179652
  67.5 21.0 %copy-start.2 = (f32[3,512,1024]{1,2,0:T(8,128)}, f32[3,512,1024]{1,2,0:T(8,128)S(1)}, u32[]{:S(2)}) copy-start(f32[3,512,1024]{1,2,0:T(8,128)S(1)} %get-tuple-element.196) | copy-start | bytes 18874372
  68.9 21.7 %copy-start = (f32[3,512,1024]{1,2,0:T(8,128)}, f32[3,512,1024]{1,2,0:T(8,128)S(1)}, u32[]{:S(2)}) copy-start(f32[3,512,1024]{1,2,0:T(8,128)S(1)} %get-tuple-element.198) | copy-start | bytes 18874372
  121.2 11.5 %copy-start.79 = (bf16[576,1536]{1,0:T(8,128)(2,1)S(1)}, bf16[576,1536]{1,0:T(8,128)(2,1)}, u32[]{:S(2)}) copy-start(bf16[576,1536]{1,0:T(8,128)(2,1)} %all-gather.4.cloned.1.call-done) | copy-start | bytes 5308420
  142.3 10.9 %copy-start.36 = (bf16[1024,576]{0,1:T(8,128)(2,1)}, bf16[1024,576]{0,1:T(8,128)(2,1)S(1)}, u32[]{:S(2)}) copy-start(bf16[1024,576]{0,1:T(8,128)(2,1)S(1)} %convolution_convert_fusion.3) | copy-start | bytes 3538948
  155.1 10.5 %copy-start.58 = (bf16[1024,192]{0,1:T(8,128)(2,1)S(1)}, bf16[1024,192]{0,1:T(8,128)(2,1)}, u32[]{:S(2)}) copy-start(bf16[1024,192]{0,1:T(8,128)(2,1)} %copy-done.56) | copy-start | bytes 1179652
  158.2 14.3 %slice-start = ((s8[6291456]{0:T(1024)(128)(4,1)}), s8[2097152]{0:T(1024)(128)(4,1)S(1)}, s32[]{:S(2)}) async-start(s8[6291456]{0:T(1024)(128)(4,1)} %bitcast.471), calls=%async_computation.17 | async-start | bytes 4194304
  165.6 6.8 %slice-start.1 = ((s8[6291456]{0:T(1024)(128)(4,1)}), s8[4194304]{0:T(1024)(128)(4,1)S(1)}, s32[]{:S(2)}) async-start(s8[6291456]{0:T(1024)(128)(4,1)} %bitcast.471), calls=%async_computation.18 | async-start | bytes 8388608
  165.6 6.8 %copy-start.37 = (bf16[1024,576]{0,1:T(8,128)(2,1)S(1)}, bf16[1024,576]{0,1:T(8,128)(2,1)}, u32[]{:S(2)}) copy-start(bf16[1024,576]{0,1:T(8,128)(2,1)} %copy-done.36) | copy-start | bytes 3538948
  172.5 9.7 %slice-start.6 = ((s8[6291456]{0:T(1024)(128)(4,1)}), s8[4194304]{0:T(1024)(128)(4,1)S(1)}, s32[]{:S(2)}) async-start(s8[6291456]{0:T(1024)(128)(4,1)} %bitcast.477), calls=%async_computation.23 | async-start | bytes 8388608
  172.5 12.4 %slice-start.4 = ((s8[6291456]{0:T(1024)(128)(4,1)}), s8[4194304]{0:T(1024)(128)(4,1)S(1)}, s32[]{:S(2)}) async-start(s8[6291456]{0:T(1024)(128)(4,1)} %bitcast.475), calls=%async_computation.21 | async-start | bytes 8388608
  175.4 6.8 %slice-start.7 = ((s8[6291456]{0:T(1024)(128)(4,1)}), s8[2097152]{0:T(1024)(128)(4,1)S(1)}, s32[]{:S(2)}) async-start(s8[6291456]{0:T(1024)(128)(4,1)} %bitcast.477), calls=%async_computation.24 | async-start | bytes 4194304
  175.4 9.5 %slice-start.5 = ((s8[6291456]{0:T(1024)(128)(4,1)}), s8[2097152]{0:T(1024)(128)(4,1)S(1)}, s32[]{:S(2)}) async-start(s8[6291456]{0:T(1024)(128)(4,1)} %bitcast.475), calls=%async_computation.22 | async-start | bytes 4194304
  188.9 5.0 copy-start.23
  195.1 103.4 %reduce-scatter.10.cloned.1.call-start = ((), (), s32[]{:S(2)}) async-start(), calls=%async_computation.11 | async-start | bytes 442368 | tf_op jit(solution)/shard_map/reduce_scatter | solution.py:331
  205.7 14.9 %copy-start.18 = (bf16[3,512,512]{1,2,0:T(8,128)(2,1)}, bf16[3,512,512]{1,2,0:T(8,128)(2,1)S(1)}, u32[]{:S(2)}) copy-start(bf16[3,512,512]{1,2,0:T(8,128)(2,1)S(1)} %fusion.27) | copy-start | bytes 4718596
  213.8 6.7 %copy-start.13 = (f32[1024,3,64]{0,2,1:T(8,128)}, f32[1024,3,64]{0,2,1:T(8,128)S(1)}, u32[]{:S(2)}) copy-start(f32[1024,3,64]{0,2,1:T(8,128)S(1)} %scatter-add.44) | copy-start | bytes 2359300
  213.8 9.0 %slice-start.8 = ((s8[6291456]{0:T(1024)(128)(4,1)}), s8[4194304]{0:T(1024)(128)(4,1)S(1)}, s32[]{:S(2)}) async-start(s8[6291456]{0:T(1024)(128)(4,1)} %bitcast.479), calls=%async_computation.25 | async-start | bytes 8388608
  213.8 9.0 %slice-start.9 = ((s8[6291456]{0:T(1024)(128)(4,1)}), s8[2097152]{0:T(1024)(128)(4,1)S(1)}, s32[]{:S(2)}) async-start(s8[6291456]{0:T(1024)(128)(4,1)} %bitcast.479), calls=%async_computation.26 | async-start | bytes 4194304
  222.9 7.2 %slice-start.2 = ((s8[6291456]{0:T(1024)(128)(4,1)}), s8[4194304]{0:T(1024)(128)(4,1)S(1)}, s32[]{:S(2)}) async-start(s8[6291456]{0:T(1024)(128)(4,1)} %bitcast.473), calls=%async_computation.19 | async-start | bytes 8388608
  222.9 7.2 %slice-start.3 = ((s8[6291456]{0:T(1024)(128)(4,1)}), s8[2097152]{0:T(1024)(128)(4,1)S(1)}, s32[]{:S(2)}) async-start(s8[6291456]{0:T(1024)(128)(4,1)} %bitcast.473), calls=%async_computation.20 | async-start | bytes 4194304
  246.5 51.9 %reduce-scatter.14.cloned.1.call-start = ((), (), s32[]{:S(2)}) async-start(), calls=%async_computation.13 | async-start | bytes 1105920 | tf_op jit(solution)/shard_map/reduce_scatter | solution.py:337
  253.4 45.1 %reduce-scatter.8.cloned.1.call-start = ((), (), s32[]{:S(2)}) async-start(), calls=%async_computation.10 | async-start | bytes 1105920 | tf_op jit(solution)/shard_map/reduce_scatter | solution.py:328
  260.4 68.3 %reduce-scatter.20.cloned.1.call-start = ((), (), s32[]{:S(2)}) async-start(), calls=%async_computation.16 | async-start | bytes 2654208 | tf_op jit(solution)/shard_map/reduce_scatter | solution.py:349
  260.5 5.6 %copy-start.49 = (bf16[1024,576]{0,1:T(8,128)(2,1)S(1)}, bf16[1024,576]{0,1:T(8,128)(2,1)}, u32[]{:S(2)}) copy-start(bf16[1024,576]{0,1:T(8,128)(2,1)} %multiply_convert_fusion.3) | copy-start | bytes 3538948
  266.1 93.9 %reduce-scatter.16.cloned.1.call-start = ((), (), s32[]{:S(2)}) async-start(), calls=%async_computation.14 | async-start | bytes 2654208 | tf_op jit(solution)/shard_map/reduce_scatter | solution.py:343
  271.5 6.0 %copy-start.43 = (bf16[1024,3,64]{0,2,1:T(8,128)(2,1)S(1)}, bf16[1024,3,64]{0,2,1:T(8,128)(2,1)}, u32[]{:S(2)}) copy-start(bf16[1024,3,64]{0,2,1:T(8,128)(2,1)} %copy-done.42) | copy-start | bytes 1179652
  271.5 6.0 %copy-start.48 = (bf16[576,192]{1,0:T(8,128)(2,1)S(1)}, bf16[576,192]{1,0:T(8,128)(2,1)}, u32[]{:S(2)}) copy-start(bf16[576,192]{1,0:T(8,128)(2,1)} %copy-done.47) | copy-start | bytes 663556
  271.5 119.4 %reduce-scatter.18.cloned.1.call-start = ((), (), s32[]{:S(2)}) async-start(), calls=%async_computation.15 | async-start | bytes 2654208 | tf_op jit(solution)/shard_map/reduce_scatter | solution.py:346
  279.8 10.2 %copy-start.68 = (f32[1024]{0:T(1024)S(1)}, f32[1024]{0:T(1024)}, u32[]{:S(2)}) copy-start(f32[1024]{0:T(1024)} %copy-done.67) | copy-start | bytes 12292
  279.8 10.2 %copy-start.30 = (f32[1024,576]{0,1:T(8,128)S(1)}, f32[1024,576]{0,1:T(8,128)}, u32[]{:S(2)}) copy-start(f32[1024,576]{0,1:T(8,128)} %copy-done.29) | copy-start | bytes 7077892
  293.5 97.4 %copy-start.71 = (f32[288]{0:T(512)S(1)}, f32[288]{0:T(512)}, u32[]{:S(2)}) copy-start(f32[288]{0:T(512)} %dynamic-slice_convert_fusion.1) | copy-start | bytes 3460
  293.5 97.4 %copy-start.72 = (f32[288]{0:T(512)S(1)}, f32[288]{0:T(512)}, u32[]{:S(2)}) copy-start(f32[288]{0:T(512)} %dynamic-slice_convert_fusion) | copy-start | bytes 3460
  (55 other events, 141.1 us)
Sparse Core Ops, SparseCore 0:
  9.6 41.1 all-gather.5
  52.4 37.5 all-gather.3
  91.5 29.6 all-gather.7
  195.2 12.0 reduce-scatter.11
  246.7 12.0 reduce-scatter.9
  260.9 16.8 reduce-scatter.13
  280.7 16.8 reduce-scatter.7
  300.5 28.2 reduce-scatter.19
  331.7 28.2 reduce-scatter.15
  362.6 28.2 reduce-scatter.17
where the time goes:
time: 568 us; the launch traced here: 562 us
  blocking collectives  222 us (39%)
  matrix products  147 us (26%)
  waiting for transfers between devices  105 us (18%)
  other arithmetic  41.8 us (7%)
  local copies, waits for them, and re-layouts  28.3 us (5%)
  between operations  17.4 us (3%)
    psum x1, blocking collectives, local(): lax.psum((owned[0], owned[1], owned[2], owned[3], owned[4], owned[5], own...  164 us
    reduce_scatter x1, waiting for transfers between devices, local(): lax.psum_scatter(grad_gate_w.astype(jnp.bfloat16), 'shard', scatter_dimen...  31.2 us
    reduce_scatter x1, waiting for transfers between devices, local(): lax.psum_scatter(grad_up_w.astype(jnp.bfloat16), 'shard', scatter_dimensi...  30.9 us
    reduce_scatter x1, waiting for transfers between devices, local(): lax.psum_scatter(grad_down_w.astype(jnp.bfloat16), 'shard', scatter_dimen...  30.3 us
    dot_general x7, matrix products, outer_sum(): lax.dot_general(left, right, (((0,), (0,)), ((), ())), preferred_element_...  24.7 us
    dot_general x6, matrix products, attend_back(): jnp.einsum('rha,ka->hrk', grad_rows, value_heads[:finish, kv_group], pref...  24.4 us
    dot_general x7, matrix products, times_transpose(): lax.dot_general(left, right, (((1,), (1,)), ((), ())), preferred_element_...  22 us
    convert_element_type x6, other arithmetic, attend_back(): grad_scores = (probability * (grad_probs - row_delta)).astype(jnp.bfloat16)  20.7 us
  transfers between devices with their start and end apart: 10, of which 4 were waited for; matrix products, arithmetic and copies ran while one was open for 24% of the time, Pallas kernels for 0%

commit v1 on v0

v1 whole, which is shorter than its diff:
```python
import functools
import math

import jax
import jax.numpy as jnp
import numpy as np
from jax import lax
from jax.experimental import pallas as pl
from jax.experimental.pallas import tpu as pltpu
from jax.sharding import PartitionSpec as P

QUERY_HEADS = 9
KEY_VALUE_HEADS = 3
HEAD_SIZE = 64
HALF = HEAD_SIZE // 2
GROUP = QUERY_HEADS // KEY_VALUE_HEADS
EPS = 1e-05
THETA = 100000.0
BF = jnp.bfloat16
F32 = jnp.float32
BLOCK = 256
VMEM_LIMIT = 56 * 2**20
AXES = ("shard", "replica")


def nn(a, b):
    return lax.dot_general(a, b, (((1,), (0,)), ((), ())), preferred_element_type=F32)


def nt(a, b):
    return lax.dot_general(a, b, (((1,), (1,)), ((), ())), preferred_element_type=F32)


def tn(a, b):
    return lax.dot_general(a, b, (((0,), (0,)), ((), ())), preferred_element_type=F32)


def whole():
    return pl.BlockSpec(memory_space=pltpu.VMEM)


def call(kernel, name, outs, flops, grid=None, in_specs=None, out_specs=None, scratch=()):
    return pl.pallas_call(
        kernel,
        name=name,
        out_shape=outs,
        grid=grid or (),
        in_specs=in_specs,
        out_specs=out_specs,
        scratch_shapes=list(scratch),
        compiler_params=pltpu.CompilerParams(vmem_limit_bytes=VMEM_LIMIT),
        cost_estimate=pl.CostEstimate(flops=flops, bytes_accessed=8 * 2**20, transcendentals=0),
    )


def shape(*dims, dtype=BF):
    return jax.ShapeDtypeStruct(dims, dtype)


def tables(count):
    inverse = np.exp(np.arange(HALF, dtype=np.float32) * np.float32(-2.0 * math.log(THETA) / HEAD_SIZE))
    angles = jnp.arange(count, dtype=jnp.int32).astype(F32)[None, :] * jnp.asarray(inverse)[:, None]
    return jnp.cos(angles), jnp.sin(angles)


def qkv_kernel(x_ref, gain_ref, w_ref, cos_ref, sin_ref, n_ref, q_ref, k_ref, v_ref):
    count = x_ref.shape[1]
    gain = gain_ref[...]
    for at in range(0, count, BLOCK):
        cols = slice(at, at + BLOCK)
        x = x_ref[:, cols].astype(F32)
        r = lax.rsqrt(jnp.mean(x * x, axis=0, keepdims=True) + EPS)
        n_ref[:, cols] = (x * r * gain).astype(BF)
    width_q = q_ref.shape[0]
    width_k = k_ref.shape[0]
    for at in range(0, count, BLOCK):
        cols = slice(at, at + BLOCK)
        y = tn(w_ref[...], n_ref[:, cols])
        c = cos_ref[:, cols]
        s = sin_ref[:, cols]
        for head in range((width_q + width_k) // HEAD_SIZE):
            row = head * HEAD_SIZE
            u1 = y[row : row + HALF]
            u2 = y[row + HALF : row + HEAD_SIZE]
            a = u1 * c - u2 * s
            b = u2 * c + u1 * s
            if row < width_q:
                a = a.astype(BF).astype(F32) * 0.125
                b = b.astype(BF).astype(F32) * 0.125
                q_ref[row : row + HALF, cols] = a.astype(BF)
                q_ref[row + HALF : row + HEAD_SIZE, cols] = b.astype(BF)
            else:
                row -= width_q
                k_ref[row : row + HALF, cols] = a.astype(BF)
                k_ref[row + HALF : row + HEAD_SIZE, cols] = b.astype(BF)
        v_ref[:, cols] = y[width_q + width_k :].astype(BF)


def causal(s, diagonal):
    low = s.shape[0] - diagonal
    rows = lax.broadcasted_iota(jnp.int32, (diagonal, s.shape[1]), 0)
    cols = lax.broadcasted_iota(jnp.int32, (diagonal, s.shape[1]), 1)
    last = jnp.where(rows <= cols, s[low:], -1e30)
    return last if low == 0 else jnp.concatenate([s[:low], last], axis=0)


def attend_kernel(q_ref, k_ref, v_ref, o_ref, lse_ref):
    count = q_ref.shape[1]
    keys = k_ref[...].astype(F32).T.astype(BF)
    for head in range(GROUP):
        rows = slice(head * HEAD_SIZE, (head + 1) * HEAD_SIZE)
        for at in range(0, count, BLOCK):
            end = at + BLOCK
            cols = slice(at, end)
            s = causal(nn(keys[:end], q_ref[rows, cols]), BLOCK)
            top = jnp.max(s, axis=0, keepdims=True)
            p = jnp.exp(s - top)
            total = jnp.sum(p, axis=0, keepdims=True)
            o = nn(v_ref[:, :end], p.astype(BF))
            o_ref[rows, cols] = (o / total).astype(BF)
            lse_ref[0, head : head + 1, cols] = top + jnp.log(total)


def middle_kernel(x_ref, heads_ref, w_ref, gain_ref, mid_ref, n_ref):
    count = x_ref.shape[1]
    gain = gain_ref[...]
    for at in range(0, count, BLOCK):
        cols = slice(at, at + BLOCK)
        m = x_ref[:, cols].astype(F32) + tn(w_ref[...], heads_ref[:, cols])
        r = lax.rsqrt(jnp.mean(m * m, axis=0, keepdims=True) + EPS)
        mid_ref[:, cols] = m
        n_ref[:, cols] = (m * r * gain).astype(BF)


def norm_back(x, gain, grad):
    r = lax.rsqrt(jnp.mean(x * x, axis=0, keepdims=True) + EPS)
    scaled = gain * grad
    dot = jnp.mean(scaled * x, axis=0, keepdims=True)
    return r * scaled - x * (r * r * r * dot)


def mlp_kernel(n_ref, cot_ref, mid_ref, gain_ref, heads_ref, wo_ref, wg_ref, wu_ref, wd_ref,
               gd_ref, gg_ref, gu_ref, out_ref, gmid_ref, gheads_ref, gwo_ref, acc_ref, gn_ref):
    step = pl.program_id(0)
    count = n_ref.shape[1]
    n = n_ref[...]
    cot = cot_ref[...]
    wg, wu, wd = wg_ref[...], wu_ref[...], wd_ref[...]
    gate = tn(wg, n)
    up = tn(wu, n)
    gh = tn(wd, cot)
    sig = 1.0 / (1.0 + jnp.exp(-gate))
    act = gate * sig
    hidden = (act * up).astype(BF)
    gup = (gh * act).astype(BF)
    ggate = (gh * up * (sig * (1.0 + gate * (1.0 - sig)))).astype(BF)
    gd_ref[...] = nt(cot, hidden).astype(BF)
    gg_ref[...] = nt(n, ggate).astype(BF)
    gu_ref[...] = nt(n, gup).astype(BF)
    part = nn(wd, hidden)
    gpart = nn(wg, ggate) + nn(wu, gup)

    @pl.when(step == 0)
    def _():
        acc_ref[...] = part
        gn_ref[...] = gpart

    @pl.when(step > 0)
    def _():
        acc_ref[...] += part
        gn_ref[...] += gpart

    @pl.when(step == pl.num_programs(0) - 1)
    def _():
        gain = gain_ref[...]
        for at in range(0, count, BLOCK):
            cols = slice(at, at + BLOCK)
            mid = mid_ref[:, cols]
            out_ref[:, cols] = (mid + acc_ref[:, cols]).astype(BF)
            gm = cot_ref[:, cols].astype(F32) + norm_back(mid, gain, gn_ref[:, cols])
            gmid_ref[:, cols] = gm
            gheads_ref[:, cols] = nn(wo_ref[...], gm.astype(BF)).astype(BF)
        gwo_ref[...] = nt(heads_ref[...], gmid_ref[...].astype(BF)).astype(BF)


def attend_back_kernel(q_ref, k_ref, v_ref, o_ref, lse_ref, go_ref, cos_ref, sin_ref,
                       gq_ref, gk_ref, gv_ref, dk_ref, dv_ref):
    count = q_ref.shape[1]
    keys = k_ref[...].astype(F32).T.astype(BF)
    values = v_ref[...].astype(F32).T.astype(BF)
    dk_ref[...] = jnp.zeros_like(dk_ref)
    dv_ref[...] = jnp.zeros_like(dv_ref)
    for head in range(GROUP):
        rows = slice(head * HEAD_SIZE, (head + 1) * HEAD_SIZE)
        for at in range(0, count, BLOCK):
            end = at + BLOCK
            cols = slice(at, end)
            q = q_ref[rows, cols]
            go = go_ref[rows, cols]
            delta = jnp.sum(go.astype(F32) * o_ref[rows, cols].astype(F32), axis=0, keepdims=True)
            s = causal(nn(keys[:end], q), BLOCK)
            p = jnp.exp(s - lse_ref[0, head : head + 1, cols])
            ds = (p * (nn(values[:end], go) - delta)).astype(BF)
            dv_ref[:, :end] += nt(go, p.astype(BF))
            dk_ref[:, :end] += nt(q, ds)
            dq = nn(k_ref[:, :end], ds) * 0.125
            c = cos_ref[:, cols]
            sn = sin_ref[:, cols]
            g1, g2 = dq[:HALF], dq[HALF:]
            gq_ref[head * HEAD_SIZE : head * HEAD_SIZE + HALF, cols] = (g1 * c + g2 * sn).astype(BF)
            gq_ref[head * HEAD_SIZE + HALF : (head + 1) * HEAD_SIZE, cols] = (g2 * c - g1 * sn).astype(BF)
    c = cos_ref[...]
    sn = sin_ref[...]
    g1, g2 = dk_ref[:HALF], dk_ref[HALF:]
    gk_ref[:HALF] = (g1 * c + g2 * sn).astype(BF)
    gk_ref[HALF:] = (g2 * c - g1 * sn).astype(BF)
    gv_ref[...] = dv_ref[...].astype(BF)


def weight_kernel(n_ref, gq_ref, gk_ref, gv_ref, out_ref):
    wq = gq_ref.shape[0]
    wk = gk_ref.shape[0]
    n = n_ref[...]
    g = jnp.concatenate([gq_ref[...], gk_ref[...], gv_ref[...]], axis=0)
    out_ref[...] = nt(n, g).astype(BF)


def tokens_kernel(x_ref, gain_ref, w_ref, gq_ref, gk_ref, gv_ref, gmid_ref, out_ref):
    count = x_ref.shape[1]
    gain = gain_ref[...]
    for at in range(0, count, BLOCK):
        cols = slice(at, at + BLOCK)
        g = jnp.concatenate([gq_ref[:, cols], gk_ref[:, cols], gv_ref[:, cols]], axis=0)
        gn = nn(w_ref[...], g)
        x = x_ref[:, cols].astype(F32)
        out_ref[:, cols] = (gmid_ref[:, cols] + norm_back(x, gain, gn)).astype(BF)


class Grid:
    def __init__(self, shards, replicas):
        self.shards, self.replicas = shards, replicas
        self.shard = lax.axis_index("shard")
        self.replica = lax.axis_index("replica")
        self.bits = [1 << i for i in range(1, replicas.bit_length() - 1)]

    def swap(self, a, shard=0, bit=0):
        pairs = []
        for s in range(self.shards):
            for r in range(self.replicas):
                pairs.append((s * self.replicas + r, (s ^ shard) * self.replicas + (r ^ bit)))
        return lax.ppermute(a, AXES, pairs)

    def side(self, bit):
        return (self.replica // bit) % 2


def pick(a, index):
    return lax.dynamic_index_in_dim(a, index, 0, keepdims=False)


def joined(side, mine, other, axis):
    return jnp.where(
        side == 0, jnp.concatenate([mine, other], axis), jnp.concatenate([other, mine], axis)
    )


def gather(grid, own, split, axis):
    side = grid.side(1)
    size = own.shape[split] // 2
    half = lax.dynamic_slice_in_dim(own, side * size, size, split)
    first = grid.swap(half, shard=1)
    second = grid.swap(first, bit=1)
    other = joined(side, first, second, split)
    return joined(grid.shard, own, other, axis)


def add(a, b):
    return (a.astype(F32) + b.astype(F32)).astype(BF)


def total(grid, grads):
    side = grid.side(1)
    a = add(pick(grads, side), grid.swap(pick(grads, 1 - side), bit=1))
    a = add(pick(a, grid.shard), grid.swap(pick(a, 1 - grid.shard), shard=1))
    bits = grid.bits[1:] + grid.bits[:1]
    split = []
    for bit in bits:
        rows = a.shape[0]
        if bit != bits[-1] and rows % 16 == 0:
            two = a.reshape(2, rows // 2, *a.shape[1:])
            mine = grid.side(bit)
            a = add(pick(two, mine), grid.swap(pick(two, 1 - mine), bit=bit))
            split.append(bit)
        else:
            a = add(a, grid.swap(a, bit=bit))
    for bit in reversed(split):
        a = joined(grid.side(bit), a, grid.swap(a, bit=bit), 0)
    other = grid.swap(a, bit=1)
    return jnp.where(side == 0, jnp.stack([a, other]), jnp.stack([other, a]))


def local(shards, replicas, tokens, cotangent, lengths, attn_gain, w_query, key_projection,
          value_projection, w_out, mlp_gain, w_gate, w_up, w_down):
    grid = Grid(shards, replicas)
    count, width = tokens.shape
    rows = w_query.shape[0]
    ff = w_gate.shape[1]
    wide_k = key_projection.shape[1]
    wide = width + 2 * wide_k
    x = tokens.T
    cot = cotangent.T
    cos, sin = tables(count)
    own_qkv = jnp.concatenate([w_query, key_projection, value_projection], axis=1)
    own_down = w_down.T
    gains = lax.all_gather(jnp.stack([attn_gain, mlp_gain]), "shard", axis=1, tiled=True).astype(F32)
    gain_one = gains[0][:, None]
    gain_two = gains[1][:, None]
    w_qkv = gather(grid, own_qkv, 0, 0)
    w_o = gather(grid, w_out, 0, 0)
    w_g = gather(grid, w_gate, 0, 0)
    w_u = gather(grid, w_up, 0, 0)
    w_d = gather(grid, own_down, 0, 1)

    normed, q, k, v = call(
        qkv_kernel, "qkv", [shape(width, count), shape(width, count), shape(wide_k, count), shape(wide_k, count)],
        2 * count * width * wide, in_specs=[whole()] * 5, out_specs=[whole()] * 4,
    )(x, gain_one, w_qkv, cos, sin)

    group = GROUP * HEAD_SIZE
    block_q = pl.BlockSpec((group, count), lambda i: (i, 0))
    block_k = pl.BlockSpec((HEAD_SIZE, count), lambda i: (i, 0))
    block_l = pl.BlockSpec((1, 8, count), lambda i: (i, 0, 0))
    block_t = pl.BlockSpec((HALF, count), lambda i: (0, 0))
    heads, lse = call(
        attend_kernel, "attend", [shape(width, count), shape(KEY_VALUE_HEADS, 8, count, dtype=F32)],
        2 * count * count * width, grid=(KEY_VALUE_HEADS,), in_specs=[block_q, block_k, block_k],
        out_specs=[block_q, block_l],
    )(q, k, v)

    middle, normed_two = call(
        middle_kernel, "middle", [shape(width, count, dtype=F32), shape(width, count)],
        2 * count * width * width, in_specs=[whole()] * 4, out_specs=[whole()] * 2,
    )(x, heads, w_o, gain_two)

    def fixed(*dims):
        return pl.BlockSpec(dims, lambda i: (0,) * len(dims))

    act = fixed(width, count)
    col = fixed(width, 1)
    square = fixed(width, width)
    block_w = pl.BlockSpec((width, BLOCK), lambda i: (0, i))
    g_down, g_gate, g_up, out, g_mid, g_heads, g_out = call(
        mlp_kernel, "mlp",
        [shape(width, ff), shape(width, ff), shape(width, ff), shape(width, count),
         shape(width, count, dtype=F32), shape(width, count), shape(width, width)],
        18 * count * width * ff, grid=(ff // BLOCK,),
        in_specs=[act, act, act, col, act, square, block_w, block_w, block_w],
        out_specs=[block_w, block_w, block_w, act, act, act, square],
        scratch=[pltpu.VMEM((width, count), F32), pltpu.VMEM((width, count), F32)],
    )(normed_two, cot, middle, gain_two, heads, w_o, w_g, w_u, w_d)

    g_q, g_k, g_v = call(
        attend_back_kernel, "attend_back", [shape(width, count), shape(wide_k, count), shape(wide_k, count)],
        5 * count * count * width, grid=(KEY_VALUE_HEADS,),
        in_specs=[block_q, block_k, block_k, block_q, block_l, block_q, block_t, block_t],
        out_specs=[block_q, block_k, block_k],
        scratch=[pltpu.VMEM((HEAD_SIZE, count), F32), pltpu.VMEM((HEAD_SIZE, count), F32)],
    )(q, k, v, heads, lse, g_heads, cos, sin)

    g_qkv = call(
        weight_kernel, "weights", shape(width, wide), 2 * count * width * wide,
        in_specs=[whole()] * 4, out_specs=whole(),
    )(normed, g_q, g_k, g_v)
    grad_tokens = call(
        tokens_kernel, "grad_tokens", shape(width, count), 2 * count * width * wide,
        in_specs=[whole()] * 7, out_specs=whole(),
    )(x, gain_one, w_qkv, g_q, g_k, g_v, g_mid)

    half_ff = ff // 2
    def by_rows(g):
        return g.reshape(2, rows, 2, g.shape[1] // 2).transpose(2, 0, 1, 3)

    t_gate = total(grid, by_rows(g_gate))
    t_up = total(grid, by_rows(g_up))
    t_down = total(grid, g_down.reshape(2, width // 2, 2, half_ff).transpose(0, 2, 1, 3))
    t_out = total(grid, by_rows(g_out))
    t_qkv = total(grid, by_rows(g_qkv))

    def rows_back(t):
        return t.transpose(1, 0, 2).reshape(rows, -1).astype(F32)

    t_gate, t_up, t_out, t_qkv = (rows_back(t) for t in (t_gate, t_up, t_out, t_qkv))
    t_down = t_down.reshape(width, half_ff).astype(F32)
    grad_attn_gain = jnp.sum(own_qkv.astype(F32) * t_qkv, axis=1) / attn_gain.astype(F32)
    grad_mlp_gain = jnp.sum(
        w_gate.astype(F32) * t_gate + w_up.astype(F32) * t_up, axis=1
    ) / mlp_gain.astype(F32)
    return (
        out.T,
        grad_tokens.T,
        grad_attn_gain,
        t_qkv[:, :width],
        t_qkv[:, width : width + wide_k],
        t_qkv[:, width + wide_k :],
        t_out,
        grad_mlp_gain,
        t_gate,
        t_up,
        t_down.T,
    )


def solution(mesh):
    tokens = P(AXES, None)
    split = P("shard", None)
    gain = P("shard")
    return jax.shard_map(
        functools.partial(local, mesh.shape["shard"], mesh.shape["replica"]),
        mesh=mesh,
        in_specs=(tokens, tokens, tokens, gain, split, split, split, split, gain, split, split, split),
        out_specs=(tokens, tokens, gain, split, split, split, split, gain, split, split, split),
        check_vma=False,
    )
```

time: 568 us -> 335 us (0.59)
  blocking collectives: 222 us -> 31.8 us
  matrix products: 147 us -> 0 us
  Pallas kernels: 0 us -> 90.3 us
  waiting for transfers between devices: 105 us -> 40.6 us
  starting transfers between devices: 0.65 us -> 54.2 us
  local copies, waits for them, and re-layouts: 28.3 us -> 70.1 us
  between operations: 17.4 us -> 1.86 us
    psum x1 -> x0, blocking collectives: 164 us -> none  [local(): lax.psum((owned[0], owned[1], owned[2], owned[3], owned[4], owned[5], own...]
    dot_general x57 -> x0, matrix products: 147 us -> none  [the longest x7 24.7 us: outer_sum(): lax.dot_general(left, right, (((0,), (0,)), ((), ())), preferred_element_...]
    reduce_scatter x7 -> x0, waiting for transfers between devices: 92.4 us -> none  [the longest x1 31.2 us: local(): lax.psum_scatter(grad_gate_w.astype(jnp.bfloat16), 'shard', scatter_dimen...]
    pallas_call x0 -> x7, Pallas kernels: none -> 90.3 us  [the longest x1 32.2 us: local(): call(mlp_kernel, 'mlp', [shape(width, ff), shape(width, ff), shape(width,...]
    ppermute x0 -> x50, starting transfers between devices: none -> 54.2 us  [swap(): return lax.ppermute(a, AXES, pairs)]
    ppermute x0 -> x50, waiting for transfers between devices: none -> 40.6 us  [swap(): return lax.ppermute(a, AXES, pairs)]
    reshape x0 -> x5, local copies, waits for them, and re-layouts: none -> 26.6 us  [the longest x1 15.4 us: local(): g_down.reshape(2, width // 2, 2, half_ff).transpose(0, 2, 1, 3)]
    select_n x0 -> x26, other arithmetic: none -> 20.3 us  [the longest x25 20.2 us: joined(): jnp.where(side == 0, jnp.concatenate([mine, other], axis), jnp.concatenat...]
  transfers between devices with their start and end apart: 10 -> 50, of which waited for: 4 -> 12; matrix products, arithmetic and copies ran while one was open for 24% -> 29% of each run, Pallas kernels for 0% -> 18%
where the time goes in v1:
time: 335 us; the launch traced here: 330 us
  Pallas kernels  90.3 us (27%)
  local copies, waits for them, and re-layouts  70.1 us (21%)
  starting transfers between devices  54.2 us (16%)
  other arithmetic  40.6 us (12%)
  waiting for transfers between devices  40.6 us (12%)
  blocking collectives  31.8 us (9%)
    ppermute x50, starting transfers between devices, swap(): return lax.ppermute(a, AXES, pairs)  54.2 us
    ppermute x50, waiting for transfers between devices, swap(): return lax.ppermute(a, AXES, pairs)  40.6 us
    pallas_call x1, Pallas kernels, local(): call(mlp_kernel, 'mlp', [shape(width, ff), shape(width, ff), shape(width,...  32.2 us
    all_gather x1, blocking collectives, local(): lax.all_gather(jnp.stack([attn_gain, mlp_gain]), 'shard', axis=1, tiled=T...  31.8 us
    select_n x25, other arithmetic, joined(): jnp.where(side == 0, jnp.concatenate([mine, other], axis), jnp.concatenat...  20.2 us
    pallas_call x1, Pallas kernels, local(): call(attend_kernel, 'attend', [shape(width, count), shape(KEY_VALUE_HEADS...  18.4 us
    pallas_call x1, Pallas kernels, local(): call(attend_back_kernel, 'attend_back', [shape(width, count), shape(wide_...  18.4 us
    reshape x1, local copies, waits for them, and re-layouts, local(): g_down.reshape(2, width // 2, 2, half_ff).transpose(0, 2, 1, 3)  15.4 us
  transfers between devices with their start and end apart: 50, of which 12 were waited for; matrix products, arithmetic and copies ran while one was open for 29% of the time, Pallas kernels for 18%

profile of v1, /device:TPU:1, one launch (start us, length us, event | category | flops | bytes accessed | tf_op | source)
XLA Modules:
  0.0 329.5 jit_solution(11585715716005556467)
XLA Ops:
  2.2 2.1 collective-permute-start
  4.3 1.6 constant_dynamic-slice_fusion.12
  11.9 31.8 %all-gather = bf16[2,288,2]{1,2,0:T(2,128)(2,1)S(1)} all-gather(bf16[1,288,2]{1,2,0:T(2,128)(2,1)S(1)} %maximum_bitcast_fusion), channel_id=1, replica_groups=mesh['shard'=2,'replica'=16] {'shard'}, dimensions={0}, use_global_device_ids=true | all-gather | bytes 3456 | tf_op jit(solution)/shard_map/all_gather | solution.py:315
  43.8 2.0 multiply_sine_fusion
  50.1 2.2 maximum_select_fusion.10.w_ref.wo_ref
  54.7 1.6 maximum_select_fusion.3.w_ref
  56.3 5.6 %qkv.1 = (bf16[576,1024]{1,0:T(8,128)(2,1)}, bf16[576,1024]{1,0:T(8,128)(2,1)}, bf16[192,1024]{1,0:T(8,128)(2,1)}, bf16[192,1024]{1,0:T(8,128)(2,1)}) custom-call(bf16[576,1024]{1,0:T(8,128)(2,1)} %bitcast.184, f32[576,1]{1,0:T(8,128)} %copy.63.gain_ref, bf16[576,960]{1,0:T(8,128)(2,1)} %maximum_select_fusion.3.w_ref, f32[32,1024]{1,0:T(8,128)} %get-tuple-element.62.cos_ref, ...), custom_call_target="tpu_custom_call" | custom-call | flops 1132462080 | bytes 8388608 | tf_op jit(solution)/shard_map/qkv/pallas_call | solution.py:324
  61.9 18.4 %attend.1 = (bf16[576,1024]{1,0:T(8,128)(2,1)}, f32[3,8,1024]{2,1,0:T(8,128)}) custom-call(bf16[576,1024]{1,0:T(8,128)(2,1)} %get-tuple-element.29.q_ref, bf16[192,1024]{1,0:T(8,128)(2,1)} %get-tuple-element.30.k_ref, bf16[192,1024]{1,0:T(8,128)(2,1)} %get-tuple-element.31.v_ref), custom_call_target="tpu_custom_call" | custom-call | flops 1207959552 | bytes 8388608 | tf_op jit(solution)/shard_map/attend/pallas_call | solution.py:334
  80.3 5.0 %middle.1 = (f32[576,1024]{1,0:T(8,128)}, bf16[576,1024]{1,0:T(8,128)(2,1)}) custom-call(bf16[576,1024]{1,0:T(8,128)(2,1)} %bitcast.185, bf16[576,1024]{1,0:T(8,128)(2,1)} %get-tuple-element.32.heads_ref.o_ref, bf16[576,576]{1,0:T(8,128)(2,1)} %maximum_select_fusion.10.w_ref.wo_ref, f32[576,1]{1,0:T(8,128)} %copy.64.gain_ref), custom_call_target="tpu_custom_call" | custom-call | flops 679477248 | bytes 8388608 | tf_op jit(solution)/shard_map/middle/pallas_call | solution.py:340
  86.7 1.9 maximum_select_fusion.wg_ref
  90.0 1.9 maximum_select_fusion.1.wu_ref
  93.3 1.6 maximum_select_fusion.2.wd_ref
  94.9 32.2 %mlp.1 = (bf16[576,1536]{1,0:T(8,128)(2,1)}, bf16[576,1536]{1,0:T(8,128)(2,1)}, bf16[576,1536]{1,0:T(8,128)(2,1)}, bf16[576,1024]{1,0:T(8,128)(2,1)}, f32[576,10...) custom-call(bf16[576,1024]{1,0:T(8,128)(2,1)} %get-tuple-element.33.n_ref, ...), custom_call_target="tpu_custom_call" | custom-call | flops 16307453952 | bytes 8388608 | tf_op jit(solution)/shard_map/mlp/pallas_call | solution.py:352
  127.1 2.5 reshape.668
  129.6 1.8 constant_dynamic-slice_fusion.7
  132.4 2.4 reshape.680
  134.8 15.4 %reshape.677 = bf16[2,288,2,768]{3,2,1,0:T(2,128)(2,1)S(1)} reshape(bf16[576,1536]{1,0:T(8,128)(2,1)} %get-tuple-element.46) | data formatting | bytes 3538944 | tf_op jit(solution)/shard_map/reshape | solution.py:385
  150.2 2.1 constant_dynamic-slice_fusion.1
  154.9 1.5 collective-permute-start.19
  156.5 18.4 %attend_back.1 = (bf16[576,1024]{1,0:T(8,128)(2,1)}, bf16[192,1024]{1,0:T(8,128)(2,1)}, bf16[192,1024]{1,0:T(8,128)(2,1)}) custom-call(bf16[576,1024]{1,0:T(8,128)(2,1)} %get-tuple-element.29.q_ref, bf16[192,1024]{1,0:T(8,128)(2,1)} %get-tuple-element.30.k_ref, bf16[192,1024]{1,0:T(8,128)(2,1)} %get-tuple-element.31.v_ref, ...), custom_call_target="tpu_custom_call" | custom-call | flops 3019898880 | bytes 8388608 | tf_op jit(solution)/shard_map/attend_back/pallas_call | solution.py:362
  174.9 4.3 %weights.1 = bf16[576,960]{1,0:T(8,128)(2,1)} custom-call(bf16[576,1024]{1,0:T(8,128)(2,1)} %get-tuple-element.42.n_ref, bf16[576,1024]{1,0:T(8,128)(2,1)} %get-tuple-element.38.gq_ref, bf16[192,1024]{1,0:T(8,128)(2,1)} %get-tuple-element.39.gk_ref, bf16[192,1024]{1,0:T(8,128)(2,1)} %get-tuple-element.40.gv_ref), custom_call_target="tpu_custom_call" | custom-call | flops 1132462080 | bytes 8388608 | tf_op jit(solution)/shard_map/weights/pallas_call | solution.py:370
  179.2 4.3 %reshape.665 = bf16[2,288,2,480]{3,2,1,0:T(2,128)(2,1)S(1)} reshape(bf16[576,960]{1,0:T(8,128)(2,1)} %weights.1) | data formatting | bytes 2211840 | tf_op jit(solution)/shard_map/reshape | solution.py:381
  186.1 3.8 %constant_dynamic-slice_fusion.9 = (bf16[2,288,1,480]{3,2,1,0:T(2,128)(2,1)}, bf16[2,288,1,480]{3,2,1,0:T(2,128)(2,1)}) fusion(bf16[2,288,2,480]{3,2,1,0:T(2,128)(2,1)S(1)} %reshape.665, s32[]{:T(128)S(6)} %select_n.470, s32[]{:T(128)S(6)} %select_n.471), kind=kLoop, calls=%fused_computation.120 | loop fusion | bytes 2211848 | tf_op jit(solution)/shard_map/dynamic-slice.1
  190.4 4.0 %reshape.674 = bf16[2,288,2,768]{3,2,1,0:T(2,128)(2,1)S(1)} reshape(bf16[576,1536]{1,0:T(8,128)(2,1)} %get-tuple-element.45) | data formatting | bytes 3538944 | tf_op jit(solution)/shard_map/reshape | solution.py:381
  197.5 2.4 collective-permute-start.21
  199.9 7.5 %constant_dynamic-slice_fusion.3 = (bf16[2,288,1,768]{3,2,1,0:T(2,128)(2,1)S(1)}, bf16[2,288,1,768]{3,2,1,0:T(2,128)(2,1)S(1)}, bf16[2,288,1,768]{3,2,1,0:T(2,128)(2,1)S(1)}, bf16[2,288,1,768]{3,2,1,0:T(2,128)(2,1)S(1)}) fusion(bf16[2,288,2,768]{3,2,1,0:T(2,128)(2,1)S(1)} %reshape.674, s32[]{:T(128)S(6)} %select_n.470, s32[]{:T(128)S(6)} %select_n.471, ...), kind=kLoop, calls=%fused_computation.114 | loop fusion | bytes 7077896 | tf_op jit(solution)/shard_map/dynamic-slice.7
  210.8 1.5 collective-permute-done.22
  212.8 4.0 %collective-permute-done.23 = bf16[72,288]{1,0:T(8,128)(2,1)S(1)} collective-permute-done((bf16[72,288]{1,0:T(8,128)(2,1)S(1)}, bf16[72,288]{1,0:T(8,128)(2,1)S(1)}, u32[]{:S(2)}, u32[]{:S(2)}) %collective-permute-start.23) | collective-permute-done | bytes 41504 | tf_op jit(solution)/shard_map/ppermute | solution.py:251
  216.9 6.4 %grad_tokens.1 = bf16[576,1024]{1,0:T(8,128)(2,1)} custom-call(bf16[576,1024]{1,0:T(8,128)(2,1)} %bitcast.186, f32[576,1]{1,0:T(8,128)} %copy.63.gain_ref, bf16[576,960]{1,0:T(8,128)(2,1)} %maximum_select_fusion.3.w_ref, bf16[576,1024]{1,0:T(8,128)(2,1)} %get-tuple-element.38.gq_ref, bf16[192,1024]{1,0:T(8,128)(2,1)} %get-tuple-element.39.gk_ref, ...), custom_call_target="tpu_custom_call" | custom-call | flops 1132462080 | bytes 8388608 | tf_op jit(solution)/shard_map/grad_tokens/pallas_call | solution.py:374
  223.4 2.7 collective-permute-start.25
  226.3 1.8 collective-permute-start.12
  230.5 1.8 collective-permute-done.12
  232.6 3.9 %collective-permute-done.13 = bf16[72,480]{1,0:T(8,128)(2,1)S(1)} collective-permute-done((bf16[72,480]{1,0:T(8,128)(2,1)S(1)}, bf16[72,480]{1,0:T(8,128)(2,1)S(1)}, u32[]{:S(2)}, u32[]{:S(2)}) %collective-permute-start.13) | collective-permute-done | bytes 69152 | tf_op jit(solution)/shard_map/ppermute | solution.py:251
  240.5 3.8 %collective-permute-done.15 = bf16[72,480]{1,0:T(8,128)(2,1)S(1)} collective-permute-done((bf16[72,480]{1,0:T(8,128)(2,1)S(1)}, bf16[72,480]{1,0:T(8,128)(2,1)S(1)}, u32[]{:S(2)}, u32[]{:S(2)}) %collective-permute-start.15) | collective-permute-done | bytes 69152 | tf_op jit(solution)/shard_map/ppermute | solution.py:251
  251.7 5.9 %collective-permute-start.17 = (bf16[288,480]{1,0:T(8,128)(2,1)S(1)}, bf16[288,480]{1,0:T(8,128)(2,1)S(1)}, u32[]{:S(2)}, u32[]{:S(2)}) collective-permute-start(bf16[288,480]{1,0:T(8,128)(2,1)S(1)} %maximum_select_fusion.22), channel_id=1, source_target_pairs={{0,1},{1,0},{2,3},{3,2},{4,5},{5,4},{6,7},{7,6},{8,9},{9,8},{10,11... | collective-permute-start | bytes 829448 | tf_op jit(solution)/shard_map/ppermute | solution.py:251
  264.0 3.1 collective-permute-done.44
  267.9 5.1 %collective-permute-done.28 = bf16[144,768]{1,0:T(8,128)(2,1)S(1)} collective-permute-done((bf16[144,768]{1,0:T(8,128)(2,1)S(1)}, bf16[144,768]{1,0:T(8,128)(2,1)S(1)}, u32[]{:S(2)}, u32[]{:S(2)}) %collective-permute-start.28) | collective-permute-done | bytes 221216 | tf_op jit(solution)/shard_map/ppermute | solution.py:251
  273.9 5.2 %collective-permute-done.36 = bf16[144,768]{1,0:T(8,128)(2,1)S(1)} collective-permute-done((bf16[144,768]{1,0:T(8,128)(2,1)S(1)}, bf16[144,768]{1,0:T(8,128)(2,1)S(1)}, u32[]{:S(2)}, u32[]{:S(2)}) %collective-permute-start.36) | collective-permute-done | bytes 221216 | tf_op jit(solution)/shard_map/ppermute | solution.py:251
  283.9 1.6 fusion.4
  292.8 2.4 collective-permute-start.47
  295.3 1.6 collective-permute-start.31
  296.9 2.4 collective-permute-start.39
  299.4 7.6 %collective-permute-done.31 = bf16[72,768]{1,0:T(8,128)(2,1)S(1)} collective-permute-done((bf16[72,768]{1,0:T(8,128)(2,1)S(1)}, bf16[72,768]{1,0:T(8,128)(2,1)S(1)}, u32[]{:S(2)}, u32[]{:S(2)}) %collective-permute-start.31) | collective-permute-done | bytes 110624 | tf_op jit(solution)/shard_map/ppermute | solution.py:251
  307.1 2.5 collective-permute-done.39
  309.9 6.2 %collective-permute-start.49 = (bf16[288,768]{1,0:T(8,128)(2,1)S(1)}, bf16[288,768]{1,0:T(8,128)(2,1)S(1)}, u32[]{:S(2)}, u32[]{:S(2)}) collective-permute-start(bf16[288,768]{1,0:T(8,128)(2,1)S(1)} %maximum_select_fusion.19), channel_id=1, source_target_pairs={{0,1},{1,0},{2,3},{3,2},{4,5},{5,4},{6,7},{7,6},{8,9},{9,8},{10,11... | collective-permute-start | bytes 1327112 | tf_op jit(solution)/shard_map/ppermute | solution.py:251
  316.2 4.6 %collective-permute-start.33 = (bf16[288,768]{1,0:T(8,128)(2,1)S(1)}, bf16[288,768]{1,0:T(8,128)(2,1)S(1)}, u32[]{:S(2)}, u32[]{:S(2)}) collective-permute-start(bf16[288,768]{1,0:T(8,128)(2,1)S(1)} %maximum_select_fusion.15), channel_id=1, source_target_pairs={{0,1},{1,0},{2,3},{3,2},{4,5},{5,4},{6,7},{7,6},{8,9},{9,8},{10,11... | collective-permute-start | bytes 1327112 | tf_op jit(solution)/shard_map/ppermute | solution.py:251
  320.9 2.3 collective-permute-start.41
  324.0 1.6 convert_bitcast_fusion
  (230 shorter events, 71.3 us)
Async XLA Ops:
  2.2 44.7 %collective-permute-start = (bf16[144,960]{1,0:T(8,128)(2,1)S(1)}, bf16[144,960]{1,0:T(8,128)(2,1)}, u32[]{:S(2)}, u32[]{:S(2)}) collective-permute-start(bf16[144,960]{1,0:T(8,128)(2,1)S(1)} %constant_dynamic-slice_fusion.13), channel_id=1, source_target_pairs={{0,16},{1,17},{2,18},{3,19},{4,20},{5,21},{6,22},{7,23},{8,24},{9,... | collective-permute-start | bytes 829448 | tf_op jit(solution)/shard_map/ppermute | solution.py:251
  5.9 39.9 %collective-permute-start.2 = (bf16[144,576]{1,0:T(8,128)(2,1)}, bf16[144,576]{1,0:T(8,128)(2,1)}, u32[]{:S(2)}, u32[]{:S(2)}) collective-permute-start(bf16[144,576]{1,0:T(8,128)(2,1)} %constant_dynamic-slice_fusion.12), channel_id=1, source_target_pairs={{0,16},{1,17},{2,18},{3,19},{4,20},{5,21},{6,22},{7,23},{8,24},{9,... | collective-permute-start | bytes 497672 | tf_op jit(solution)/shard_map/ppermute | solution.py:251
  6.7 45.5 %collective-permute-start.4 = (bf16[144,1536]{1,0:T(8,128)(2,1)}, bf16[144,1536]{1,0:T(8,128)(2,1)}, u32[]{:S(2)}, u32[]{:S(2)}) collective-permute-start(bf16[144,1536]{1,0:T(8,128)(2,1)} %constant_dynamic-slice_fusion.11), channel_id=1, source_target_pairs={{0,16},{1,17},{2,18},{3,19},{4,20},{5,21},{6,22},{7,23},{8,24},{9,... | collective-permute-start | bytes 1327112 | tf_op jit(solution)/shard_map/ppermute | solution.py:251
  9.0 43.7 %collective-permute-start.6 = (bf16[144,1536]{1,0:T(8,128)(2,1)}, bf16[144,1536]{1,0:T(8,128)(2,1)}, u32[]{:S(2)}, u32[]{:S(2)}) collective-permute-start(bf16[144,1536]{1,0:T(8,128)(2,1)} %constant_dynamic-slice_fusion.10), channel_id=1, source_target_pairs={{0,16},{1,17},{2,18},{3,19},{4,20},{5,21},{6,22},{7,23},{8,24},{9,... | collective-permute-start | bytes 1327112 | tf_op jit(solution)/shard_map/ppermute | solution.py:251
  9.8 43.0 %collective-permute-start.8 = (bf16[288,768]{1,0:T(8,128)(2,1)}, bf16[288,768]{1,0:T(8,128)(2,1)}, u32[]{:S(2)}, u32[]{:S(2)}) collective-permute-start(bf16[288,768]{1,0:T(8,128)(2,1)} %dynamic-slice_bitcast_fusion.3), channel_id=1, source_target_pairs={{0,16},{1,17},{2,18},{3,19},{4,20},{5,21},{6,22},{7,23},{8,24},{9,... | collective-permute-start | bytes 1327112 | tf_op jit(solution)/shard_map/ppermute | solution.py:251
  46.9 6.4 %collective-permute-start.1 = (bf16[144,960]{1,0:T(8,128)(2,1)}, bf16[144,960]{1,0:T(8,128)(2,1)}, u32[]{:S(2)}, u32[]{:S(2)}) collective-permute-start(bf16[144,960]{1,0:T(8,128)(2,1)} %collective-permute-done), channel_id=1, source_target_pairs={{0,1},{1,0},{2,3},{3,2},{4,5},{5,4},{6,7},{7,6},{8,9},{9,8},{10,11... | collective-permute-start | bytes 829448 | tf_op jit(solution)/shard_map/ppermute | solution.py:251
  52.2 33.1 %collective-permute-start.5 = (bf16[144,1536]{1,0:T(8,128)(2,1)}, bf16[144,1536]{1,0:T(8,128)(2,1)S(1)}, u32[]{:S(2)}, u32[]{:S(2)}) collective-permute-start(bf16[144,1536]{1,0:T(8,128)(2,1)} %collective-permute-done.4), channel_id=1, source_target_pairs={{0,1},{1,0},{2,3},{3,2},{4,5},{5,4},{6,7},{7,6},{8,9},{9,8},{10,11... | collective-permute-start | bytes 1327112 | tf_op jit(solution)/shard_map/ppermute | solution.py:251
  52.7 35.9 %collective-permute-start.7 = (bf16[144,1536]{1,0:T(8,128)(2,1)}, bf16[144,1536]{1,0:T(8,128)(2,1)S(1)}, u32[]{:S(2)}, u32[]{:S(2)}) collective-permute-start(bf16[144,1536]{1,0:T(8,128)(2,1)} %collective-permute-done.6), channel_id=1, source_target_pairs={{0,1},{1,0},{2,3},{3,2},{4,5},{5,4},{6,7},{7,6},{8,9},{9,8},{10,11... | collective-permute-start | bytes 1327112 | tf_op jit(solution)/shard_map/ppermute | solution.py:251
  52.8 39.1 %collective-permute-start.9 = (bf16[288,768]{1,0:T(8,128)(2,1)}, bf16[288,768]{1,0:T(8,128)(2,1)S(1)}, u32[]{:S(2)}, u32[]{:S(2)}) collective-permute-start(bf16[288,768]{1,0:T(8,128)(2,1)} %collective-permute-done.8), channel_id=1, source_target_pairs={{0,1},{1,0},{2,3},{3,2},{4,5},{5,4},{6,7},{7,6},{8,9},{9,8},{10,11... | collective-permute-start | bytes 1327112 | tf_op jit(solution)/shard_map/ppermute | solution.py:251
  132.3 21.5 %collective-permute-start.18 = (bf16[2,288,288]{2,1,0:T(8,128)(2,1)}, bf16[2,288,288]{2,1,0:T(8,128)(2,1)}, u32[]{:S(2)}, u32[]{:S(2)}) collective-permute-start(bf16[2,288,288]{2,1,0:T(8,128)(2,1)} %bitcast.179), channel_id=1, source_target_pairs={{0,1},{1,0},{2,3},{3,2},{4,5},{5,4},{6,7},{7,6},{8,9},{9,8},{10,11... | collective-permute-start | bytes 995336 | tf_op jit(solution)/shard_map/ppermute | solution.py:251
  153.3 74.7 %collective-permute-start.42 = (bf16[2,288,768]{2,1,0:T(8,128)(2,1)}, bf16[2,288,768]{2,1,0:T(8,128)(2,1)}, u32[]{:S(2)}, u32[]{:S(2)}) collective-permute-start(bf16[2,288,768]{2,1,0:T(8,128)(2,1)} %bitcast.175), channel_id=1, source_target_pairs={{0,1},{1,0},{2,3},{3,2},{4,5},{5,4},{6,7},{7,6},{8,9},{9,8},{10,11... | collective-permute-start | bytes 2654216 | tf_op jit(solution)/shard_map/ppermute | solution.py:251
  154.9 28.5 %collective-permute-start.19 = (bf16[288,288]{1,0:T(8,128)(2,1)S(1)}, bf16[288,288]{1,0:T(8,128)(2,1)S(1)}, u32[]{:S(2)}, u32[]{:S(2)}) collective-permute-start(bf16[288,288]{1,0:T(8,128)(2,1)S(1)} %dynamic-slice_bitcast_fusion.8), channel_id=1, source_target_pairs={{0,16},{1,17},{2,18},{3,19},{4,20},{5,21},{6,22},{7,23},{8,24},{9,... | collective-permute-start | bytes 497672 | tf_op jit(solution)/shard_map/ppermute | solution.py:251
  184.9 11.7 %collective-permute-start.20 = (bf16[144,288]{1,0:T(8,128)(2,1)}, bf16[144,288]{1,0:T(8,128)(2,1)}, u32[]{:S(2)}, u32[]{:S(2)}) collective-permute-start(bf16[144,288]{1,0:T(8,128)(2,1)} %dynamic-slice_bitcast_fusion.13), channel_id=1, source_target_pairs={{0,4},{1,5},{2,6},{3,7},{4,0},{5,1},{6,2},{7,3},{8,12},{9,13},{10,... | collective-permute-start | bytes 248840 | tf_op jit(solution)/shard_map/ppermute | solution.py:251
  195.9 14.7 %collective-permute-start.10 = (bf16[2,288,480]{2,1,0:T(8,128)(2,1)S(1)}, bf16[2,288,480]{2,1,0:T(8,128)(2,1)S(1)}, u32[]{:S(2)}, u32[]{:S(2)}) collective-permute-start(bf16[2,288,480]{2,1,0:T(8,128)(2,1)S(1)} %bitcast.215), channel_id=1, source_target_pairs={{0,1},{1,0},{2,3},{3,2},{4,5},{5,4},{6,7},{7,6},{8,9},{9,8},{10,11... | collective-permute-start | bytes 1658888 | tf_op jit(solution)/shard_map/ppermute | solution.py:251
  197.5 11.7 %collective-permute-start.21 = (bf16[72,288]{1,0:T(8,128)(2,1)S(1)}, bf16[72,288]{1,0:T(8,128)(2,1)S(1)}, u32[]{:S(2)}, u32[]{:S(2)}) collective-permute-start(bf16[72,288]{1,0:T(8,128)(2,1)S(1)} %dynamic-slice_bitcast_fusion.15), channel_id=1, source_target_pairs={{0,8},{1,9},{2,10},{3,11},{4,12},{5,13},{6,14},{7,15},{8,0},{9,1},... | collective-permute-start | bytes 124424 | tf_op jit(solution)/shard_map/ppermute | solution.py:251
  207.6 24.8 %collective-permute-start.26 = (bf16[2,288,768]{2,1,0:T(8,128)(2,1)S(1)}, bf16[2,288,768]{2,1,0:T(8,128)(2,1)S(1)}, u32[]{:S(2)}, u32[]{:S(2)}) collective-permute-start(bf16[2,288,768]{2,1,0:T(8,128)(2,1)S(1)} %bitcast.214), channel_id=1, source_target_pairs={{0,1},{1,0},{2,3},{3,2},{4,5},{5,4},{6,7},{7,6},{8,9},{9,8},{10,11... | collective-permute-start | bytes 2654216 | tf_op jit(solution)/shard_map/ppermute | solution.py:251
  209.0 31.3 %collective-permute-start.34 = (bf16[2,288,768]{2,1,0:T(8,128)(2,1)}, bf16[2,288,768]{2,1,0:T(8,128)(2,1)S(1)}, u32[]{:S(2)}, u32[]{:S(2)}) collective-permute-start(bf16[2,288,768]{2,1,0:T(8,128)(2,1)} %bitcast.176), channel_id=1, source_target_pairs={{0,1},{1,0},{2,3},{3,2},{4,5},{5,4},{6,7},{7,6},{8,9},{9,8},{10,11... | collective-permute-start | bytes 2654216 | tf_op jit(solution)/shard_map/ppermute | solution.py:251
  212.3 4.4 %collective-permute-start.23 = (bf16[72,288]{1,0:T(8,128)(2,1)S(1)}, bf16[72,288]{1,0:T(8,128)(2,1)S(1)}, u32[]{:S(2)}, u32[]{:S(2)}) collective-permute-start(bf16[72,288]{1,0:T(8,128)(2,1)S(1)} %add_convert_fusion.4), channel_id=1, source_target_pairs={{0,8},{1,9},{2,10},{3,11},{4,12},{5,13},{6,14},{7,15},{8,0},{9,1},... | collective-permute-start | bytes 124424 | tf_op jit(solution)/shard_map/ppermute | solution.py:251
  212.5 13.7 %collective-permute-start.11 = (bf16[288,480]{1,0:T(8,128)(2,1)S(1)}, bf16[288,480]{1,0:T(8,128)(2,1)S(1)}, u32[]{:S(2)}, u32[]{:S(2)}) collective-permute-start(bf16[288,480]{1,0:T(8,128)(2,1)S(1)} %dynamic-slice_bitcast_fusion.4), channel_id=1, source_target_pairs={{0,16},{1,17},{2,18},{3,19},{4,20},{5,21},{6,22},{7,23},{8,24},{9,... | collective-permute-start | bytes 829448 | tf_op jit(solution)/shard_map/ppermute | solution.py:251
  216.8 6.5 %collective-permute-start.24 = (bf16[144,288]{1,0:T(8,128)(2,1)S(1)}, bf16[144,288]{1,0:T(8,128)(2,1)S(1)}, u32[]{:S(2)}, u32[]{:S(2)}) collective-permute-start(bf16[144,288]{1,0:T(8,128)(2,1)S(1)} %maximum_select_fusion.29), channel_id=1, source_target_pairs={{0,4},{1,5},{2,6},{3,7},{4,0},{5,1},{6,2},{7,3},{8,12},{9,13},{10,... | collective-permute-start | bytes 248840 | tf_op jit(solution)/shard_map/ppermute | solution.py:251
  223.4 24.1 %collective-permute-start.25 = (bf16[288,288]{1,0:T(8,128)(2,1)S(1)}, bf16[288,288]{1,0:T(8,128)(2,1)S(1)}, u32[]{:S(2)}, u32[]{:S(2)}) collective-permute-start(bf16[288,288]{1,0:T(8,128)(2,1)S(1)} %maximum_select_fusion.24), channel_id=1, source_target_pairs={{0,1},{1,0},{2,3},{3,2},{4,5},{5,4},{6,7},{7,6},{8,9},{9,8},{10,11... | collective-permute-start | bytes 497672 | tf_op jit(solution)/shard_map/ppermute | solution.py:251
  226.3 6.0 %collective-permute-start.12 = (bf16[144,480]{1,0:T(8,128)(2,1)S(1)}, bf16[144,480]{1,0:T(8,128)(2,1)S(1)}, u32[]{:S(2)}, u32[]{:S(2)}) collective-permute-start(bf16[144,480]{1,0:T(8,128)(2,1)S(1)} %dynamic-slice_bitcast_fusion.9), channel_id=1, source_target_pairs={{0,4},{1,5},{2,6},{3,7},{4,0},{5,1},{6,2},{7,3},{8,12},{9,13},{10,... | collective-permute-start | bytes 414728 | tf_op jit(solution)/shard_map/ppermute | solution.py:251
  230.2 28.6 %collective-permute-start.43 = (bf16[288,768]{1,0:T(8,128)(2,1)}, bf16[288,768]{1,0:T(8,128)(2,1)}, u32[]{:S(2)}, u32[]{:S(2)}) collective-permute-start(bf16[288,768]{1,0:T(8,128)(2,1)} %dynamic-slice_bitcast_fusion), channel_id=1, source_target_pairs={{0,16},{1,17},{2,18},{3,19},{4,20},{5,21},{6,22},{7,23},{8,24},{9,... | collective-permute-start | bytes 1327112 | tf_op jit(solution)/shard_map/ppermute | solution.py:251
  232.3 4.2 %collective-permute-start.13 = (bf16[72,480]{1,0:T(8,128)(2,1)S(1)}, bf16[72,480]{1,0:T(8,128)(2,1)S(1)}, u32[]{:S(2)}, u32[]{:S(2)}) collective-permute-start(bf16[72,480]{1,0:T(8,128)(2,1)S(1)} %dynamic-slice_bitcast_fusion.14), channel_id=1, source_target_pairs={{0,8},{1,9},{2,10},{3,11},{4,12},{5,13},{6,14},{7,15},{8,0},{9,1},... | collective-permute-start | bytes 207368 | tf_op jit(solution)/shard_map/ppermute | solution.py:251
  236.5 3.7 %collective-permute-start.14 = (bf16[72,480]{1,0:T(8,128)(2,1)S(1)}, bf16[72,480]{1,0:T(8,128)(2,1)S(1)}, u32[]{:S(2)}, u32[]{:S(2)}) collective-permute-start(bf16[72,480]{1,0:T(8,128)(2,1)S(1)} %fusion.19), channel_id=1, source_target_pairs={{0,2},{1,3},{2,0},{3,1},{4,6},{5,7},{6,4},{7,5},{8,10},{9,11},{10,... | collective-permute-start | bytes 207368 | tf_op jit(solution)/shard_map/ppermute | solution.py:251
  238.6 21.5 %collective-permute-start.27 = (bf16[288,768]{1,0:T(8,128)(2,1)}, bf16[288,768]{1,0:T(8,128)(2,1)}, u32[]{:S(2)}, u32[]{:S(2)}) collective-permute-start(bf16[288,768]{1,0:T(8,128)(2,1)} %dynamic-slice_bitcast_fusion.2), channel_id=1, source_target_pairs={{0,16},{1,17},{2,18},{3,19},{4,20},{5,21},{6,22},{7,23},{8,24},{9,... | collective-permute-start | bytes 1327112 | tf_op jit(solution)/shard_map/ppermute | solution.py:251
  240.2 4.2 %collective-permute-start.15 = (bf16[72,480]{1,0:T(8,128)(2,1)S(1)}, bf16[72,480]{1,0:T(8,128)(2,1)S(1)}, u32[]{:S(2)}, u32[]{:S(2)}) collective-permute-start(bf16[72,480]{1,0:T(8,128)(2,1)S(1)} %add_convert_fusion.3), channel_id=1, source_target_pairs={{0,8},{1,9},{2,10},{3,11},{4,12},{5,13},{6,14},{7,15},{8,0},{9,1},... | collective-permute-start | bytes 207368 | tf_op jit(solution)/shard_map/ppermute | solution.py:251
  245.1 5.4 %collective-permute-start.16 = (bf16[144,480]{1,0:T(8,128)(2,1)}, bf16[144,480]{1,0:T(8,128)(2,1)}, u32[]{:S(2)}, u32[]{:S(2)}) collective-permute-start(bf16[144,480]{1,0:T(8,128)(2,1)} %maximum_select_fusion.28), channel_id=1, source_target_pairs={{0,4},{1,5},{2,6},{3,7},{4,0},{5,1},{6,2},{7,3},{8,12},{9,13},{10,... | collective-permute-start | bytes 414728 | tf_op jit(solution)/shard_map/ppermute | solution.py:251
  247.2 15.6 %collective-permute-start.35 = (bf16[288,768]{1,0:T(8,128)(2,1)}, bf16[288,768]{1,0:T(8,128)(2,1)}, u32[]{:S(2)}, u32[]{:S(2)}) collective-permute-start(bf16[288,768]{1,0:T(8,128)(2,1)} %dynamic-slice_bitcast_fusion.1), channel_id=1, source_target_pairs={{0,16},{1,17},{2,18},{3,19},{4,20},{5,21},{6,22},{7,23},{8,24},{9,... | collective-permute-start | bytes 1327112 | tf_op jit(solution)/shard_map/ppermute | solution.py:251
  251.7 28.2 %collective-permute-start.17 = (bf16[288,480]{1,0:T(8,128)(2,1)S(1)}, bf16[288,480]{1,0:T(8,128)(2,1)S(1)}, u32[]{:S(2)}, u32[]{:S(2)}) collective-permute-start(bf16[288,480]{1,0:T(8,128)(2,1)S(1)} %maximum_select_fusion.22), channel_id=1, source_target_pairs={{0,1},{1,0},{2,3},{3,2},{4,5},{5,4},{6,7},{7,6},{8,9},{9,8},{10,11... | collective-permute-start | bytes 829448 | tf_op jit(solution)/shard_map/ppermute | solution.py:251
  260.0 7.1 %collective-permute-start.44 = (bf16[144,768]{1,0:T(8,128)(2,1)S(1)}, bf16[144,768]{1,0:T(8,128)(2,1)S(1)}, u32[]{:S(2)}, u32[]{:S(2)}) collective-permute-start(bf16[144,768]{1,0:T(8,128)(2,1)S(1)} %dynamic-slice_bitcast_fusion.5), channel_id=1, source_target_pairs={{0,4},{1,5},{2,6},{3,7},{4,0},{5,1},{6,2},{7,3},{8,12},{9,13},{10,... | collective-permute-start | bytes 663560 | tf_op jit(solution)/shard_map/ppermute | solution.py:251
  261.3 11.8 %collective-permute-start.28 = (bf16[144,768]{1,0:T(8,128)(2,1)S(1)}, bf16[144,768]{1,0:T(8,128)(2,1)S(1)}, u32[]{:S(2)}, u32[]{:S(2)}) collective-permute-start(bf16[144,768]{1,0:T(8,128)(2,1)S(1)} %dynamic-slice_bitcast_fusion.7), channel_id=1, source_target_pairs={{0,4},{1,5},{2,6},{3,7},{4,0},{5,1},{6,2},{7,3},{8,12},{9,13},{10,... | collective-permute-start | bytes 663560 | tf_op jit(solution)/shard_map/ppermute | solution.py:251
  263.9 15.1 %collective-permute-start.36 = (bf16[144,768]{1,0:T(8,128)(2,1)S(1)}, bf16[144,768]{1,0:T(8,128)(2,1)S(1)}, u32[]{:S(2)}, u32[]{:S(2)}) collective-permute-start(bf16[144,768]{1,0:T(8,128)(2,1)S(1)} %dynamic-slice_bitcast_fusion.6), channel_id=1, source_target_pairs={{0,4},{1,5},{2,6},{3,7},{4,0},{5,1},{6,2},{7,3},{8,12},{9,13},{10,... | collective-permute-start | bytes 663560 | tf_op jit(solution)/shard_map/ppermute | solution.py:251
  267.9 19.1 %collective-permute-start.45 = (bf16[72,768]{1,0:T(8,128)(2,1)}, bf16[72,768]{1,0:T(8,128)(2,1)}, u32[]{:S(2)}, u32[]{:S(2)}) collective-permute-start(bf16[72,768]{1,0:T(8,128)(2,1)} %dynamic-slice_bitcast_fusion.10), channel_id=1, source_target_pairs={{0,8},{1,9},{2,10},{3,11},{4,12},{5,13},{6,14},{7,15},{8,0},{9,1},... | collective-permute-start | bytes 331784 | tf_op jit(solution)/shard_map/ppermute | solution.py:251
  273.9 15.4 %collective-permute-start.29 = (bf16[72,768]{1,0:T(8,128)(2,1)}, bf16[72,768]{1,0:T(8,128)(2,1)}, u32[]{:S(2)}, u32[]{:S(2)}) collective-permute-start(bf16[72,768]{1,0:T(8,128)(2,1)} %dynamic-slice_bitcast_fusion.12), channel_id=1, source_target_pairs={{0,8},{1,9},{2,10},{3,11},{4,12},{5,13},{6,14},{7,15},{8,0},{9,1},... | collective-permute-start | bytes 331784 | tf_op jit(solution)/shard_map/ppermute | solution.py:251
  279.9 10.7 %collective-permute-start.37 = (bf16[72,768]{1,0:T(8,128)(2,1)}, bf16[72,768]{1,0:T(8,128)(2,1)}, u32[]{:S(2)}, u32[]{:S(2)}) collective-permute-start(bf16[72,768]{1,0:T(8,128)(2,1)} %dynamic-slice_bitcast_fusion.11), channel_id=1, source_target_pairs={{0,8},{1,9},{2,10},{3,11},{4,12},{5,13},{6,14},{7,15},{8,0},{9,1},... | collective-permute-start | bytes 331784 | tf_op jit(solution)/shard_map/ppermute | solution.py:251
  288.0 4.8 %collective-permute-start.46 = (bf16[72,768]{1,0:T(8,128)(2,1)S(1)}, bf16[72,768]{1,0:T(8,128)(2,1)S(1)}, u32[]{:S(2)}, u32[]{:S(2)}) collective-permute-start(bf16[72,768]{1,0:T(8,128)(2,1)S(1)} %fusion.15), channel_id=1, source_target_pairs={{0,2},{1,3},{2,0},{3,1},{4,6},{5,7},{6,4},{7,5},{8,10},{9,11},{10,... | collective-permute-start | bytes 331784 | tf_op jit(solution)/shard_map/ppermute | solution.py:251
  290.2 5.0 %collective-permute-start.30 = (bf16[72,768]{1,0:T(8,128)(2,1)S(1)}, bf16[72,768]{1,0:T(8,128)(2,1)S(1)}, u32[]{:S(2)}, u32[]{:S(2)}) collective-permute-start(bf16[72,768]{1,0:T(8,128)(2,1)S(1)} %fusion.17), channel_id=1, source_target_pairs={{0,2},{1,3},{2,0},{3,1},{4,6},{5,7},{6,4},{7,5},{8,10},{9,11},{10,... | collective-permute-start | bytes 331784 | tf_op jit(solution)/shard_map/ppermute | solution.py:251
  291.5 5.4 %collective-permute-start.38 = (bf16[72,768]{1,0:T(8,128)(2,1)S(1)}, bf16[72,768]{1,0:T(8,128)(2,1)S(1)}, u32[]{:S(2)}, u32[]{:S(2)}) collective-permute-start(bf16[72,768]{1,0:T(8,128)(2,1)S(1)} %fusion.16), channel_id=1, source_target_pairs={{0,2},{1,3},{2,0},{3,1},{4,6},{5,7},{6,4},{7,5},{8,10},{9,11},{10,... | collective-permute-start | bytes 331784 | tf_op jit(solution)/shard_map/ppermute | solution.py:251
  292.8 6.5 %collective-permute-start.47 = (bf16[72,768]{1,0:T(8,128)(2,1)S(1)}, bf16[72,768]{1,0:T(8,128)(2,1)S(1)}, u32[]{:S(2)}, u32[]{:S(2)}) collective-permute-start(bf16[72,768]{1,0:T(8,128)(2,1)S(1)} %add_convert_fusion), channel_id=1, source_target_pairs={{0,8},{1,9},{2,10},{3,11},{4,12},{5,13},{6,14},{7,15},{8,0},{9,1},... | collective-permute-start | bytes 331784 | tf_op jit(solution)/shard_map/ppermute | solution.py:251
  295.3 11.7 %collective-permute-start.31 = (bf16[72,768]{1,0:T(8,128)(2,1)S(1)}, bf16[72,768]{1,0:T(8,128)(2,1)S(1)}, u32[]{:S(2)}, u32[]{:S(2)}) collective-permute-start(bf16[72,768]{1,0:T(8,128)(2,1)S(1)} %add_convert_fusion.2), channel_id=1, source_target_pairs={{0,8},{1,9},{2,10},{3,11},{4,12},{5,13},{6,14},{7,15},{8,0},{9,1},... | collective-permute-start | bytes 331784 | tf_op jit(solution)/shard_map/ppermute | solution.py:251
  296.9 12.7 %collective-permute-start.39 = (bf16[72,768]{1,0:T(8,128)(2,1)S(1)}, bf16[72,768]{1,0:T(8,128)(2,1)S(1)}, u32[]{:S(2)}, u32[]{:S(2)}) collective-permute-start(bf16[72,768]{1,0:T(8,128)(2,1)S(1)} %add_convert_fusion.1), channel_id=1, source_target_pairs={{0,8},{1,9},{2,10},{3,11},{4,12},{5,13},{6,14},{7,15},{8,0},{9,1},... | collective-permute-start | bytes 331784 | tf_op jit(solution)/shard_map/ppermute | solution.py:251
  299.3 10.4 %collective-permute-start.48 = (bf16[144,768]{1,0:T(8,128)(2,1)S(1)}, bf16[144,768]{1,0:T(8,128)(2,1)S(1)}, u32[]{:S(2)}, u32[]{:S(2)}) collective-permute-start(bf16[144,768]{1,0:T(8,128)(2,1)S(1)} %maximum_select_fusion.27), channel_id=1, source_target_pairs={{0,4},{1,5},{2,6},{3,7},{4,0},{5,1},{6,2},{7,3},{8,12},{9,13},{10,... | collective-permute-start | bytes 663560 | tf_op jit(solution)/shard_map/ppermute | solution.py:251
  307.0 9.0 %collective-permute-start.32 = (bf16[144,768]{1,0:T(8,128)(2,1)S(1)}, bf16[144,768]{1,0:T(8,128)(2,1)S(1)}, u32[]{:S(2)}, u32[]{:S(2)}) collective-permute-start(bf16[144,768]{1,0:T(8,128)(2,1)S(1)} %maximum_select_fusion.25), channel_id=1, source_target_pairs={{0,4},{1,5},{2,6},{3,7},{4,0},{5,1},{6,2},{7,3},{8,12},{9,13},{10,... | collective-permute-start | bytes 663560 | tf_op jit(solution)/shard_map/ppermute | solution.py:251
  309.7 11.1 %collective-permute-start.40 = (bf16[144,768]{1,0:T(8,128)(2,1)S(1)}, bf16[144,768]{1,0:T(8,128)(2,1)S(1)}, u32[]{:S(2)}, u32[]{:S(2)}) collective-permute-start(bf16[144,768]{1,0:T(8,128)(2,1)S(1)} %maximum_select_fusion.26), channel_id=1, source_target_pairs={{0,4},{1,5},{2,6},{3,7},{4,0},{5,1},{6,2},{7,3},{8,12},{9,13},{10,... | collective-permute-start | bytes 663560 | tf_op jit(solution)/shard_map/ppermute | solution.py:251
  309.9 14.0 %collective-permute-start.49 = (bf16[288,768]{1,0:T(8,128)(2,1)S(1)}, bf16[288,768]{1,0:T(8,128)(2,1)S(1)}, u32[]{:S(2)}, u32[]{:S(2)}) collective-permute-start(bf16[288,768]{1,0:T(8,128)(2,1)S(1)} %maximum_select_fusion.19), channel_id=1, source_target_pairs={{0,1},{1,0},{2,3},{3,2},{4,5},{5,4},{6,7},{7,6},{8,9},{9,8},{10,11... | collective-permute-start | bytes 1327112 | tf_op jit(solution)/shard_map/ppermute | solution.py:251
  316.2 7.3 %collective-permute-start.33 = (bf16[288,768]{1,0:T(8,128)(2,1)S(1)}, bf16[288,768]{1,0:T(8,128)(2,1)S(1)}, u32[]{:S(2)}, u32[]{:S(2)}) collective-permute-start(bf16[288,768]{1,0:T(8,128)(2,1)S(1)} %maximum_select_fusion.15), channel_id=1, source_target_pairs={{0,1},{1,0},{2,3},{3,2},{4,5},{5,4},{6,7},{7,6},{8,9},{9,8},{10,11... | collective-permute-start | bytes 1327112 | tf_op jit(solution)/shard_map/ppermute | solution.py:251
  320.9 4.8 %collective-permute-start.41 = (bf16[288,768]{1,0:T(8,128)(2,1)S(1)}, bf16[288,768]{1,0:T(8,128)(2,1)S(1)}, u32[]{:S(2)}, u32[]{:S(2)}) collective-permute-start(bf16[288,768]{1,0:T(8,128)(2,1)S(1)} %maximum_select_fusion.17), channel_id=1, source_target_pairs={{0,1},{1,0},{2,3},{3,2},{4,5},{5,4},{6,7},{7,6},{8,9},{9,8},{10,11... | collective-permute-start | bytes 1327112 | tf_op jit(solution)/shard_map/ppermute | solution.py:251
  (30 other events, 150.7 us)
